TPU v7x, 256 devices: a whole 4x4x8 slice. The times are simulated.
256 devices in a mesh: row: 16 (over z, core), col: 4 (over y), depth: 4 (over x).
Axes of the slice: x: 4, y: 4, z: 8, core: 2. Of those that a mesh axis runs over, the one named last changes fastest.
Arguments:
- a_blocks: bfloat16 [2048, 256, 256], P(('row', 'col', 'depth')), may hold values from -0.375 to 0.375
- a_scale: float32 [2048], P(('row', 'col', 'depth')), may hold values from 0.25 to 4
- a_rows: int32 [2048], P(('row', 'col', 'depth')), may hold values from -1 to 127, as said below
- a_cols: int32 [2048], P(('row', 'col', 'depth')), may hold values from 0 to 127, as said below
- b_blocks: bfloat16 [32, 4, 4, 3, 256, 256], P('row', 'col', 'depth'), may hold values from -6 to 6
- b_scale: float32 [32, 4, 4, 3], P('row', 'col', 'depth'), may hold values from 0.25 to 4
- b_cols: int32 [32, 4, 4, 3], P('row', 'col', 'depth'), may hold values from 0 to 127, as said below
- c_rows: int32 [5120], P(('row', 'col', 'depth')), may hold values from 0 to 127, as said below
- c_cols: int32 [5120], P(('row', 'col', 'depth')), may hold values from 0 to 127, as said below
Outputs:
- c_blocks: bfloat16 [5120, 256, 256], P(('row', 'col', 'depth'))
Inputs may be any that keep to these rules, and one draw needn't show every extreme that they name: `a_rows`: slots are laid out device by device in mesh order, 8 a device. A device of row index r holds blocks of block rows r * 8 to (r + 1) * 8 - 1; -1 marks an empty slot; on each device the occupied slots come first, no two occupied slots name the same block, and in every draw some device has all 8 slots occupied. `a_cols`: A device of column index c and depth index e holds blocks whose column k has k % 4 == e and (k // 4) % 4 == c, empty slots included. b_cols[g, c, e, t] lies in block columns c * 32 to (c + 1) * 32 - 1, and the 3 entries of one (g, c, e) differ. `c_rows`: slots are laid out device by device in mesh order, 20 a device. A device of row index r holds result blocks of block rows r * 8 to (r + 1) * 8 - 1; no two slots name the same block. `c_cols`: A device of column index c and depth index e holds result blocks of block columns c * 32 + e * 8 and the next 7.
All inputs are finite; a program needn't handle non-finite values.
Results may differ from a plain program's by a relative error of at most 0.0075.
Values may be sent and summed in bfloat16 or wider, within the bound.
A program may use at most 128 MiB of HBM per device.

v0:
```python
import jax
import jax.numpy as jnp
from jax import lax
from jax.sharding import PartitionSpec as P


def shards(a_blocks, a_scale, a_rows, a_cols, b_blocks, b_scale, b_cols, c_rows, c_cols):
    block_edge = a_blocks.shape[1]
    depth_count = lax.axis_size("depth")
    row_groups = b_blocks.shape[0]
    per_row = b_blocks.shape[3]
    a_tags = jnp.stack([a_scale, a_rows.astype(jnp.float32), a_cols.astype(jnp.float32)])
    a_tags_all = lax.all_gather(a_tags, "col", axis=1, tiled=True)
    a_all = lax.all_gather(a_blocks, "col", axis=0, tiled=True)
    a_weight = a_tags_all[0]
    a_target = a_tags_all[1].astype(jnp.int32)
    a_inner = a_tags_all[2].astype(jnp.int32)
    needed = a_inner // depth_count
    b_local = b_blocks.reshape(row_groups, per_row, block_edge, block_edge)
    b_tags = jnp.stack(
        [
            b_scale.reshape(row_groups, per_row),
            b_cols.reshape(row_groups, per_row).astype(jnp.float32),
        ]
    )
    b_tags_all = lax.all_gather(b_tags, "row", axis=1, tiled=True)
    b_all = lax.all_gather(b_local, "row", axis=0, tiled=True)
    chosen = b_all[needed]
    products = jnp.einsum("aij,atjk->atik", a_all, chosen, preferred_element_type=jnp.float32)
    weights = a_weight[:, None] * b_tags_all[0][needed]
    target_cols = b_tags_all[1][needed].astype(jnp.int32)
    pattern = lax.all_gather(jnp.stack([c_rows, c_cols]), "depth", axis=1, tiled=True)
    slots_out = pattern.shape[1]
    matches = (pattern[0][:, None, None] == a_target[None, :, None]) & (
        pattern[1][:, None, None] == target_cols[None]
    )
    located = jnp.any(matches, axis=0)
    target = jnp.argmax(matches, axis=0)
    segment = jnp.where(located, target, slots_out).reshape(-1)
    weighted = (products * weights[:, :, None, None]).reshape(-1, block_edge, block_edge)
    partial_sums = jax.ops.segment_sum(weighted, segment, num_segments=slots_out + 1)[:slots_out]
    reduced = lax.psum_scatter(
        partial_sums.astype(jnp.bfloat16), "depth", scatter_dimension=0, tiled=True
    )
    return reduced


def solution(mesh):
    return jax.shard_map(
        shards,
        mesh=mesh,
        in_specs=(
            P(("row", "col", "depth"), None, None),
            P(("row", "col", "depth")),
            P(("row", "col", "depth")),
            P(("row", "col", "depth")),
            P("row", "col", "depth", None, None, None),
            P("row", "col", "depth", None),
            P("row", "col", "depth", None),
            P(("row", "col", "depth")),
            P(("row", "col", "depth")),
        ),
        out_specs=P(("row", "col", "depth"), None, None),
        check_vma=False,
    )
```

profile of v0, /device:TPU:1, one launch (start us, length us, event | category | flops | bytes accessed | tf_op | source)
XLA Modules:
  0.0 362.3 jit_solution(15614846263871254554)
XLA Ops:
  6.5 0.0 all-gather.8.cloned.1.call-start
  6.5 0.7 all-gather.8.cloned.1.call-update
  7.3 0.0 all-gather.6.cloned.1.call-start
  7.3 0.7 all-gather.6.cloned.1.call-update
  8.0 0.0 reduce-scatter.2.cloned.1.call-start
  8.1 0.7 convert_element_type.54
  8.7 0.7 pad_maximum_fusion
  9.4 0.7 add_bitcast_fusion
  10.1 8.5 %all-gather.1 = s32[4,20,2]{1,2,0:T(2,128)S(1)} all-gather(s32[1,20,2]{1,2,0:T(2,128)S(1)} %add_bitcast_fusion), channel_id=1, replica_groups=mesh['row'=16,'col'=4,'depth'=4] {'depth'}, dimensions={0}, use_global_device_ids=true | all-gather | bytes 800 | tf_op jit(solution)/shard_map/all_gather | solution.py:32
  18.6 0.1 reshape.187
  18.7 0.7 convert_bitcast_fusion.1
  19.4 0.7 maximum_bitcast_fusion
  20.1 8.9 %all-gather.2 = f32[4,8,3]{1,2,0:T(4,128)S(1)} all-gather(f32[1,8,3]{1,2,0:T(4,128)S(1)} %maximum_bitcast_fusion), channel_id=1, replica_groups=mesh['row'=16,'col'=4,'depth'=4] {'col'}, dimensions={0}, use_global_device_ids=true | all-gather | bytes 480 | tf_op jit(solution)/shard_map/all_gather | solution.py:13
  29.0 0.1 reshape.189
  29.0 24.9 %all_gather.17 = f32[2,32,3]{2,0,1:T(2,128)S(1)} all-gather(f32[2,2,3]{2,0,1:T(2,128)S(1)} %copy.47), channel_id=1, replica_groups=mesh['row'=16,'col'=4,'depth'=4] {'row'}, dimensions={1}, use_global_device_ids=true | all-gather | bytes 816 | tf_op jit(solution)/shard_map/all_gather | solution.py:26
  54.0 0.6 gather_fusion.2
  54.6 0.6 gather_fusion
  55.2 0.1 copy.50
  55.3 0.1 broadcast_compare_fusion
  55.4 0.2 fusion.1
  55.6 0.8 iota_reduce_fusion
  56.4 0.1 copy.51
  56.5 0.1 reshape.178
  56.6 0.1 broadcast_multiply_fusion.1
  56.6 32.6 %all-gather.8.cloned.1.call-done = bf16[32,1,1,3,256,256]{5,4,3,2,1,0:T(8,128)(2,1)} async-done(((bf16[2,1,1,3,256,256]{5,4,3,2,1,0:T(8,128)(2,1)}), bf16[32,1,1,3,256,256]{5,4,3,2,1,0:T(8,128)(2,1)}) %all-gather.8.cloned.1.call-update) | async-done | bytes 12582928 | tf_op jit(solution)/shard_map/all_gather | solution.py:27
  89.3 11.5 %gather_fusion.1 = bf16[32,3,256,256]{3,2,1,0:T(8,128)(2,1)} fusion(bf16[32,3,256,256]{3,2,1,0:T(8,128)(2,1)} %bitcast.56, s32[1024]{0:T(1024)S(1)} %pad_clamp_fusion), kind=kCustom, calls=%fused_computation.1 | custom fusion | bytes 25165952 | tf_op jit(solution)/shard_map/gather | solution.py:28
  100.8 39.3 %all-gather.6.cloned.1.call-done = bf16[32,256,256]{2,1,0:T(8,128)(2,1)} async-done(((bf16[8,256,256]{2,1,0:T(8,128)(2,1)}), bf16[32,256,256]{2,1,0:T(8,128)(2,1)}) %all-gather.6.cloned.1.call-update) | async-done | bytes 4194320 | tf_op jit(solution)/shard_map/all_gather | solution.py:14
  140.1 14.8 %broadcast_multiply_fusion = f32[32,3,256,256]{3,2,1,0:T(8,128)} fusion(f32[32,3]{1,0:T(8,128)S(1)} %broadcast_multiply_fusion.1, bf16[32,3,256,256]{3,2,1,0:T(8,128)(2,1)} %gather_fusion.1, bf16[32,256,256]{2,1,0:T(8,128)(2,1)} %all-gather.6.cloned.1.call-done), kind=kOutput, calls=%fused_computation.5 | convolution fusion | flops 3227516928 | bytes 41943424 | tf_op jit(solution)/shard_map/aij,atjk->atik/dot_general | solution.py:29
  154.9 24.7 %copy.55 = f32[96,256,256]{2,1,0:T(8,128)} copy(f32[96,256,256]{1,2,0:T(8,128)} %bitcast.55) | data formatting | bytes 50331648 | tf_op jit(solution)/shard_map/reshape | solution.py:40
  179.5 9.7 %broadcast_in_dim.5 = f32[81,256,256]{2,1,0:T(8,128)} broadcast(f32[]{:T(128)} %constant.20.clone.1), dimensions={} | broadcast | bytes 21233668 | tf_op jit(solution)/shard_map/broadcast_in_dim | solution.py:41
  189.2 53.1 %scatter_fusion = f32[81,256,256]{2,1,0:T(8,128)} fusion(f32[81,256,256]{2,1,0:T(8,128)} %broadcast_in_dim.5, s32[96]{0:T(128)S(1)} %reshape.178, f32[96,256,256]{2,1,0:T(8,128)} %copy.55), kind=kCustom, calls=%fused_computation.3 | custom fusion | flops 6291456 | bytes 75497856 | tf_op jit(solution)/shard_map/scatter-add | solution.py:41
  242.3 12.1 %slice.48 = bf16[80,256,256]{2,1,0:T(8,128)(2,1)} slice(f32[81,256,256]{2,1,0:T(8,128)} %scatter_fusion), slice={[0:80], [0:256], [0:256]} | slice | bytes 20971520 | tf_op jit(solution)/shard_map/slice | solution.py:41
  254.4 0.0 reduce-scatter.2.cloned.1.call-update
  254.4 101.4 %reduce-scatter.2.cloned.1.call-done = bf16[20,256,256]{2,1,0:T(8,128)(2,1)} async-done(((bf16[80,256,256]{2,1,0:T(8,128)(2,1)}), bf16[20,256,256]{2,1,0:T(8,128)(2,1)}) %reduce-scatter.2.cloned.1.call-update) | async-done | bytes 2621456 | tf_op jit(solution)/shard_map/reduce_scatter | solution.py:42
  (10 shorter events, 0.1 us)
Async XLA Ops:
  6.5 82.7 %all-gather.8.cloned.1.call-start = ((), (), s32[]{:S(2)}) async-start(), calls=%async_computation.3 | async-start | bytes 13369344 | tf_op jit(solution)/shard_map/all_gather | solution.py:27
  7.3 132.8 %all-gather.6.cloned.1.call-start = ((), (), s32[]{:S(2)}) async-start(), calls=%async_computation.1 | async-start | bytes 5242880 | tf_op jit(solution)/shard_map/all_gather | solution.py:14
  8.0 347.8 %reduce-scatter.2.cloned.1.call-start = ((), (), s32[]{:S(2)}) async-start(), calls=%async_computation.2 | async-start | bytes 13107200 | tf_op jit(solution)/shard_map/reduce_scatter | solution.py:42
Sparse Core Ops, SparseCore 0:
  9.2 80.0 all-gather.7
  91.1 48.9 all-gather.5
  254.5 101.2 reduce-scatter.1
where the time goes:
time: 363 us; the launch traced here: 362 us
  waiting for transfers between devices  175 us (48%)
  local copies, waits for them, and re-layouts  59.6 us (16%)
  other arithmetic  57.6 us (16%)
  blocking collectives  42.4 us (12%)
  matrix products  14.8 us (4%)
  between operations  13.1 us (4%)
    reduce_scatter x1, waiting for transfers between devices, shards(): lax.psum_scatter(partial_sums.astype(jnp.bfloat16), 'depth', scatter_dime...  101 us
    scatter-add x1, other arithmetic, shards(): jax.ops.segment_sum(weighted, segment, num_segments=slots_out + 1)  53.1 us
    all_gather x1, waiting for transfers between devices, shards(): a_all = lax.all_gather(a_blocks, 'col', axis=0, tiled=True)  39.3 us
    all_gather x1, waiting for transfers between devices, shards(): b_all = lax.all_gather(b_local, 'row', axis=0, tiled=True)  32.6 us
    all_gather x1, blocking collectives, shards(): b_tags_all = lax.all_gather(b_tags, 'row', axis=1, tiled=True)  24.9 us
    reshape x1, local copies, waits for them, and re-layouts, shards(): (products * weights[:, :, None, None]).reshape(-1, block_edge, block_edge)  24.7 us
    dot_general x1, matrix products, shards(): jnp.einsum('aij,atjk->atik', a_all, chosen, preferred_element_type=jnp.fl...  14.8 us
    slice x1, local copies, waits for them, and re-layouts, shards(): jax.ops.segment_sum(weighted, segment, num_segments=slots_out + 1)  12.1 us
  transfers between devices with their start and end apart: 3, of which 3 were waited for; matrix products, arithmetic and copies ran while one was open for 5% of the time, Pallas kernels for 0%

commit v1 on v0

v1 whole, which is shorter than its diff:
```python
import functools

import jax
import jax.numpy as jnp
from jax import lax
from jax.experimental import pallas as pl
from jax.experimental.pallas import tpu as pltpu
from jax.sharding import PartitionSpec as P

MESH = pl.DeviceIdType.MESH
LANES = 128
F32 = jnp.float32


def iota(shape, dim):
    return lax.broadcasted_iota(jnp.int32, shape, dim)


def schedule(dims, meta_x, meta_y, meta_z, tab_int, tab_scale):
    n_x, n_y, n_r, a_cap, per, kb, c_cap = dims
    eye = iota((a_cap, LANES), 0) == iota((a_cap, LANES), 1)

    def column(which):
        parts = [
            jnp.sum(jnp.where(eye, meta_y[c, which : which + 1, :], 0.0), axis=1, keepdims=True)
            for c in range(n_y)
        ]
        return jnp.concatenate(parts, axis=0)

    a_scale, a_rows, a_cols = column(0), column(1), column(2)
    n_a = n_y * a_cap
    group = a_cols.astype(jnp.int32) // n_x
    device, inner = group // per, group % per
    lane = iota((n_a, LANES), 1)
    b_scale = jnp.zeros((n_a, LANES), F32)
    b_cols = jnp.zeros((n_a, LANES), F32)
    for d in range(n_r):
        here = device == d
        b_scale = jnp.where(here, meta_z[d, 3:4, :], b_scale)
        b_cols = jnp.where(here, meta_z[d, 4:5, :], b_cols)
    slots, weights, a_ids, b_ids = [], [], [], []
    n_slots = n_x * c_cap
    for t in range(kb):
        pick = lane == inner * kb + t
        col = jnp.sum(jnp.where(pick, b_cols, 0.0), axis=1, keepdims=True)
        scale = jnp.sum(jnp.where(pick, b_scale, 0.0), axis=1, keepdims=True)
        found = jnp.zeros((n_a, LANES), F32)
        for e in range(n_x):
            hit = (a_rows == meta_x[e, 5:6, :]) & (col == meta_x[e, 6:7, :]) & (lane < c_cap)
            found = jnp.where(hit, (lane + (e * c_cap + 1)).astype(F32), found)
        slot = jnp.max(found, axis=1, keepdims=True)
        slots.append(jnp.where(slot > 0, slot - 1, float(n_slots)))
        weights.append(a_scale * scale)
        a_ids.append(iota((n_a, 1), 0).astype(F32))
        b_ids.append((group * kb + t).astype(F32))
    slot = jnp.concatenate(slots, axis=0)
    weight = jnp.concatenate(weights, axis=0)
    a_id = jnp.concatenate(a_ids, axis=0)
    b_id = jnp.concatenate(b_ids, axis=0)
    n_p = kb * n_a
    place, lane = iota((n_p, LANES), 0), iota((n_p, LANES), 1)
    row_slot = jnp.sum(jnp.where(place == lane, slot, 0.0), axis=0, keepdims=True)
    row_slot = jnp.where(lane[:1] < n_p, row_slot, 1e6)
    earlier = (row_slot == slot) & (lane < place)
    before = (row_slot < slot) | earlier
    rank = jnp.sum(jnp.where(before, 1.0, 0.0), axis=1, keepdims=True)
    keep = jnp.where(jnp.sum(jnp.where(earlier, 1.0, 0.0), axis=1, keepdims=True) > 0, 1.0, 0.0)
    mine = rank == lane.astype(F32)

    def ordered(values):
        return jnp.sum(jnp.where(mine, values, 0.0), axis=0, keepdims=True)

    lane_f = lane.astype(F32)
    last = jnp.sum(jnp.where(slot <= lane_f, 1.0, 0.0), axis=0, keepdims=True) - 1.0
    some = jnp.sum(jnp.where(slot == lane_f, 1.0, 0.0), axis=0, keepdims=True)
    last = jnp.where(some > 0, last, float(n_p))
    zero = jnp.zeros((1, LANES), F32)
    table = jnp.concatenate(
        [ordered(a_id), ordered(b_id), last, zero, zero, zero, zero, zero], axis=0
    ).astype(jnp.int32)
    which = iota(table.shape, 0)
    top = jnp.where(which == 0, n_a - 1, jnp.where(which == 1, n_r * per * kb - 1, n_p))
    tab_int[...] = jnp.clip(table, 0, top)
    tab_scale[...] = jnp.concatenate(
        [ordered(weight), ordered(keep), zero, zero, zero, zero, zero, zero], axis=0
    )


def kernel(
    dims, a_hbm, b_hbm, meta, out_hbm, a_all, b_all, meta_x, meta_y, meta_z, tab_int, tab_scale, ids, scales,
    acc, prod, to_right, to_left, from_left, from_right, result,
    local_sem, meta_send, meta_recv, ring_send, ring_recv, core_send, core_recv, a_send, a_recv,
    c_send_r, c_send_l, c_recv_l, c_recv_r, out_sem,
):
    n_x, n_y, n_r, a_cap, per, kb, c_cap = dims
    n_z = n_r // 2
    row, col, dep = lax.axis_index("row"), lax.axis_index("col"), lax.axis_index("depth")
    z, core = row // 2, row % 2

    def at_z(step):
        return (lax.rem(z + step + n_z, n_z) * 2 + core, col, dep)

    def at_y(step):
        return (row, lax.rem(col + step + n_y, n_y), dep)

    def at_x(step):
        return (row, col, lax.rem(dep + step + n_x, n_x))

    sibling = (z * 2 + 1 - core, col, dep)

    barrier = pltpu.get_barrier_semaphore()
    partners = [sibling, at_z(1), at_z(-1)] + [at_y(j) for j in range(1, n_y)] + [at_x(j) for j in range(1, n_x)]
    for partner in partners:
        pl.semaphore_signal(barrier, inc=1, device_id=partner, device_id_type=MESH)
    pl.semaphore_wait(barrier, len(partners))

    sends = []

    def copy(src, dst, send, recv, device):
        return pltpu.make_async_remote_copy(
            src_ref=src, dst_ref=dst, send_sem=send, recv_sem=recv, device_id=device, device_id_type=MESH
        )

    def push(src, dst, send, recv, device):
        made = copy(src, dst, send, recv, device)
        made.start()
        sends.append(made)

    def pulled(dst, send, recv):
        copy(dst, dst, send, recv, sibling).wait_recv()

    count = 0
    meta_waits = []
    for j in range(1, n_y):
        push(meta, meta_y.at[col], meta_send.at[count], meta_recv.at[count], at_y(j))
        meta_waits.append((meta_y.at[lax.rem(col - j + n_y, n_y)], count))
        count += 1
    for j in range(1, n_x):
        push(meta, meta_x.at[dep], meta_send.at[count], meta_recv.at[count], at_x(j))
        meta_waits.append((meta_x.at[lax.rem(dep - j + n_x, n_x)], count))
        count += 1
    push(meta, meta_z.at[row], meta_send.at[count], meta_recv.at[count], sibling)
    meta_waits.append((meta_z.at[z * 2 + 1 - core], count))
    count += 1
    hops_up, hops_down = n_z // 2, (n_z - 1) // 2
    ring_meta = count
    push(meta, meta_z.at[row], meta_send.at[count], meta_recv.at[count], at_z(1))
    push(meta, meta_z.at[row], meta_send.at[count + 1], meta_recv.at[count + 1], at_z(-1))
    count += 2 * hops_up
    core_meta = count

    def b_piece(origin_z, origin_core, half):
        return b_all.at[pl.ds(((origin_z * 2 + origin_core) * per + half) * kb, kb)]

    up, down = at_z(1), at_z(-1)
    half_a = a_cap // 2

    def a_piece(origin, half):
        return a_all.at[pl.ds(origin * a_cap + half * half_a, half_a)]

    def ring_slot(direction, step, half):
        return (direction * hops_up + step) * 2 + half

    for order in range(2):
        h_up, h_down = order, 1 - order
        s_up, s_down = ring_slot(0, 0, h_up), ring_slot(1, 0, h_down)
        push(b_hbm.at[h_up], b_piece(z, core, h_up), ring_send.at[s_up], ring_recv.at[s_up], up)
        push(b_hbm.at[h_down], b_piece(z, core, h_down), ring_send.at[s_down], ring_recv.at[s_down], down)
        push(a_hbm.at[pl.ds(h_up * half_a, half_a)], a_piece(col, h_up), a_send.at[order], a_recv.at[order], at_y(1))
        push(
            a_hbm.at[pl.ds(h_down * half_a, half_a)], a_piece(col, h_down), a_send.at[3 + order],
            a_recv.at[3 + order], at_y(-1),
        )
    for half in range(per):
        push(b_hbm.at[half], b_piece(z, core, half), core_send.at[half], core_recv.at[half], sibling)
    local = [
        pltpu.make_async_copy(a_hbm, a_all.at[pl.ds(col * a_cap, a_cap)], local_sem.at[0]),
        pltpu.make_async_copy(b_hbm.at[0], b_piece(z, core, 0), local_sem.at[1]),
        pltpu.make_async_copy(b_hbm.at[1], b_piece(z, core, 1), local_sem.at[2]),
    ]
    for made in local:
        made.start()
    meta_x[dep] = meta[...]
    meta_y[col] = meta[...]
    meta_z[row] = meta[...]

    def forward_meta(step):
        for direction, hops in ((0, hops_up), (1, hops_down)):
            if step >= hops:
                continue
            origin_z = lax.rem(z - step - 1 + n_z, n_z) if direction == 0 else lax.rem(z + step + 1, n_z)
            here = meta_z.at[origin_z * 2 + core]
            index = ring_meta + 2 * step + direction
            pulled(here, meta_send.at[index], meta_recv.at[index])
            if step + 1 < hops:
                push(here, here, meta_send.at[index + 2], meta_recv.at[index + 2], up if direction == 0 else down)
            push(here, here, meta_send.at[core_meta + 2 * step + direction],
                 meta_recv.at[core_meta + 2 * step + direction], sibling)
            meta_waits.append((meta_z.at[origin_z * 2 + 1 - core], core_meta + 2 * step + direction))

    core_waits = [(b_piece(z, 1 - core, half), half) for half in range(per)]

    def forward_b(step, order):
        for direction in range(2):
            half = order if direction == 0 else 1 - order
            hops = hops_up if order == 0 else hops_down
            if step >= hops:
                continue
            origin_z = lax.rem(z - step - 1 + n_z, n_z) if direction == 0 else lax.rem(z + step + 1, n_z)
            here = b_piece(origin_z, core, half)
            index = ring_slot(direction, step, half)
            pulled(here, ring_send.at[index], ring_recv.at[index])
            if step + 1 < hops:
                index = ring_slot(direction, step + 1, half)
                push(here, here, ring_send.at[index], ring_recv.at[index], up if direction == 0 else down)
            index = per + ring_slot(direction, step, half)
            push(here, here, core_send.at[index], core_recv.at[index], sibling)
            core_waits.append((b_piece(origin_z, 1 - core, half), index))

    def forward_a():
        here = a_piece(lax.rem(col + n_y - 1, n_y), 0)
        pulled(here, a_send.at[0], a_recv.at[0])
        push(here, here, a_send.at[2], a_recv.at[2], at_y(1))
        here = a_piece(lax.rem(col + 1, n_y), 1)
        pulled(here, a_send.at[3], a_recv.at[3])
        push(here, here, a_send.at[5], a_recv.at[5], at_y(-1))

    forward_meta(0)
    forward_b(0, 0)
    forward_a()
    forward_meta(1)
    forward_b(0, 1)
    forward_meta(2)
    forward_b(1, 0)
    forward_meta(3)
    forward_b(1, 1)
    for here, index in meta_waits:
        pulled(here, meta_send.at[index], meta_recv.at[index])
    schedule(dims, meta_x, meta_y, meta_z, tab_int, tab_scale)
    table = [
        pltpu.make_async_copy(tab_int, ids, local_sem.at[3]),
        pltpu.make_async_copy(tab_scale, scales, local_sem.at[4]),
    ]
    for made in table:
        made.start()
    forward_b(2, 0)
    forward_b(2, 1)
    forward_b(3, 0)
    for made in table + local:
        made.wait()
    pulled(a_piece(lax.rem(col + n_y - 1, n_y), 1), a_send.at[1], a_recv.at[1])
    pulled(a_piece(lax.rem(col + 1, n_y), 0), a_send.at[4], a_recv.at[4])
    opposite = lax.rem(col + 2, n_y)
    pulled(a_piece(opposite, 0), a_send.at[2], a_recv.at[2])
    pulled(a_piece(opposite, 1), a_send.at[5], a_recv.at[5])
    for here, index in core_waits:
        pulled(here, core_send.at[index], core_recv.at[index])

    n_p = kb * n_y * a_cap
    acc[...] = jnp.zeros_like(acc)
    prod[n_p] = jnp.zeros(prod.shape[1:], prod.dtype)

    def bounded(index, size):
        return jnp.clip(index, 0, size - 1)

    @pl.loop(0, n_p)
    def _(j):
        left_block = a_all[bounded(ids[0, j], n_y * a_cap)]
        right_block = b_all[bounded(ids[1, j], n_r * per * kb)]
        product = jnp.dot(left_block, right_block, preferred_element_type=F32)
        total = acc[...] * scales[1, j] + product * scales[0, j]
        acc[...] = total
        prod[j] = total.astype(prod.dtype)

    half_c = c_cap // 2
    piece = 2
    steps = half_c // piece
    right, left = at_x(1), at_x(-1)
    d_right, d_left, d_far = right[2], left[2], lax.rem(dep + 2, n_x)

    def own(dest, index):
        return prod[bounded(ids[2, dest * c_cap + index], n_p + 1)]

    def part(refs, stage, k):
        return refs.at[pl.ds(stage * half_c + k * piece, piece)]

    def send_right(stage, k):
        index = stage * steps + k
        return copy(part(to_right, stage, k), part(from_left, stage, k), c_send_r.at[index], c_recv_l.at[index], right)

    def send_left(stage, k):
        index = stage * steps + k
        return copy(part(to_left, stage, k), part(from_right, stage, k), c_send_l.at[index], c_recv_r.at[index], left)

    def wait_left(stage, k):
        here, index = part(from_left, stage, k), stage * steps + k
        copy(here, here, c_send_r.at[index], c_recv_l.at[index], right).wait_recv()

    def wait_right(stage, k):
        here, index = part(from_right, stage, k), stage * steps + k
        copy(here, here, c_send_l.at[index], c_recv_r.at[index], left).wait_recv()

    @pl.loop(0, steps)
    def _(k):
        for i in range(piece):
            to_right[k * piece + i] = own(d_far, k * piece + i)
        send_right(0, k).start()
        for i in range(piece):
            to_left[k * piece + i] = own(d_far, half_c + k * piece + i)
        send_left(0, k).start()

    @pl.loop(0, steps)
    def _(k):
        for i in range(piece):
            to_right[half_c + k * piece + i] = own(d_right, half_c + k * piece + i)
        send_right(1, k).start()
        for i in range(piece):
            to_left[half_c + k * piece + i] = own(d_left, k * piece + i)
        send_left(1, k).start()

    @pl.loop(0, steps)
    def _(k):
        wait_left(0, k)
        for i in range(piece):
            m = k * piece + i
            total = own(d_right, m).astype(F32) + from_left[m].astype(F32)
            to_right[2 * half_c + m] = total.astype(prod.dtype)
        send_right(2, k).start()
        wait_right(0, k)
        for i in range(piece):
            m = k * piece + i
            total = own(d_left, half_c + m).astype(F32) + from_right[m].astype(F32)
            to_left[2 * half_c + m] = total.astype(prod.dtype)
        send_left(2, k).start()

    def write(half, k):
        here = pl.ds(half * half_c + k * piece, piece)
        return pltpu.make_async_copy(result.at[here], out_hbm.at[here], out_sem.at[half * steps + k])

    @pl.loop(0, steps)
    def _(k):
        wait_right(1, k)
        wait_left(2, k)
        for i in range(piece):
            m = k * piece + i
            total = own(dep, m).astype(F32) + from_left[2 * half_c + m].astype(F32)
            result[m] = (total + from_right[half_c + m].astype(F32)).astype(prod.dtype)
        write(0, k).start()
        wait_left(1, k)
        wait_right(2, k)
        for i in range(piece):
            m = k * piece + i
            total = own(dep, half_c + m).astype(F32) + from_right[2 * half_c + m].astype(F32)
            result[half_c + m] = (total + from_left[half_c + m].astype(F32)).astype(prod.dtype)
        write(1, k).start()

    @pl.loop(0, steps)
    def _(k):
        write(0, k).wait()
        write(1, k).wait()
        for stage in range(3):
            send_right(stage, k).wait_send()
            send_left(stage, k).wait_send()

    for made in sends:
        made.wait_send()


def shards(a_blocks, a_scale, a_rows, a_cols, b_blocks, b_scale, b_cols, c_rows, c_cols):
    edge = a_blocks.shape[1]
    a_cap, c_cap = a_blocks.shape[0], c_rows.shape[0]
    per, kb = b_blocks.shape[0], b_blocks.shape[3]
    n_r, n_y, n_x = lax.axis_size("row"), lax.axis_size("col"), lax.axis_size("depth")
    dims = (n_x, n_y, n_r, a_cap, per, kb, c_cap)
    half_c = c_cap // 2
    n_p = kb * n_y * a_cap

    def line(values):
        flat = values.reshape(-1).astype(F32)
        return jnp.pad(flat, (0, LANES - flat.shape[0]))

    meta = jnp.stack([line(v) for v in (a_scale, a_rows, a_cols, b_scale, b_cols, c_rows, c_cols, c_cols)])
    dtype = a_blocks.dtype
    block = (edge, edge)
    dma = pltpu.SemaphoreType.DMA
    n_z = n_r // 2
    n_meta = (n_y - 1) + (n_x - 1) + 1 + 2 * (n_z // 2) + 2 * (n_z // 2)
    n_ring = 2 * (n_z // 2) * 2
    return pl.pallas_call(
        functools.partial(kernel, dims),
        out_shape=jax.ShapeDtypeStruct((c_cap,) + block, dtype),
        in_specs=[
            pl.BlockSpec(memory_space=pl.ANY),
            pl.BlockSpec(memory_space=pl.ANY),
            pl.BlockSpec(memory_space=pltpu.VMEM),
        ],
        out_specs=pl.BlockSpec(memory_space=pl.ANY),
        scratch_shapes=[
            pltpu.VMEM((n_y * a_cap,) + block, dtype),
            pltpu.VMEM((n_r * per * kb,) + block, dtype),
            pltpu.VMEM((n_x, 8, LANES), F32),
            pltpu.VMEM((n_y, 8, LANES), F32),
            pltpu.VMEM((n_r, 8, LANES), F32),
            pltpu.VMEM((8, LANES), jnp.int32),
            pltpu.VMEM((8, LANES), F32),
            pltpu.SMEM((8, LANES), jnp.int32),
            pltpu.SMEM((8, LANES), F32),
            pltpu.VMEM(block, F32),
            pltpu.VMEM((n_p + 1,) + block, dtype),
            pltpu.VMEM((3 * half_c,) + block, dtype),
            pltpu.VMEM((3 * half_c,) + block, dtype),
            pltpu.VMEM((3 * half_c,) + block, dtype),
            pltpu.VMEM((3 * half_c,) + block, dtype),
            pltpu.VMEM((c_cap,) + block, dtype),
            dma((5,)),
            dma((n_meta,)),
            dma((n_meta,)),
            dma((n_ring,)),
            dma((n_ring,)),
            dma((per + n_ring,)),
            dma((per + n_ring,)),
            dma((6,)),
            dma((6,)),
            dma((3 * half_c,)),
            dma((3 * half_c,)),
            dma((3 * half_c,)),
            dma((3 * half_c,)),
            dma((c_cap,)),
        ],
        compiler_params=pltpu.CompilerParams(
            collective_id=0, has_side_effects=True, vmem_limit_bytes=60 * 1024 * 1024
        ),
    )(a_blocks, b_blocks.reshape(per, kb, edge, edge), meta)


def solution(mesh):
    return jax.shard_map(
        shards,
        mesh=mesh,
        in_specs=(
            P(("row", "col", "depth"), None, None),
            P(("row", "col", "depth")),
            P(("row", "col", "depth")),
            P(("row", "col", "depth")),
            P("row", "col", "depth", None, None, None),
            P("row", "col", "depth", None),
            P("row", "col", "depth", None),
            P(("row", "col", "depth")),
            P(("row", "col", "depth")),
        ),
        out_specs=P(("row", "col", "depth"), None, None),
        check_vma=False,
    )
```

time: 363 us -> 193 us (0.53)
  Pallas kernels: 0 us -> 182 us
  waiting for transfers between devices: 175 us -> 0 us
  local copies, waits for them, and re-layouts: 59.6 us -> 5.43 us
  other arithmetic: 57.6 us -> 4.67 us
  blocking collectives: 42.4 us -> 0 us
  matrix products: 14.8 us -> 0 us
  between operations: 13.1 us -> 0.02 us
    pallas_call x0 -> x1, Pallas kernels: none -> 182 us  [shards(): pl.pallas_call(functools.partial(kernel, dims), out_shape=jax.ShapeDtypeS...]
    reduce_scatter x1 -> x0, waiting for transfers between devices: 101 us -> none  [shards(): lax.psum_scatter(partial_sums.astype(jnp.bfloat16), 'depth', scatter_dime...]
    all_gather x2 -> x0, waiting for transfers between devices: 72 us -> none  [the longest x1 39.3 us: shards(): a_all = lax.all_gather(a_blocks, 'col', axis=0, tiled=True)]
    scatter-add x1 -> x0, other arithmetic: 53.1 us -> none  [shards(): jax.ops.segment_sum(weighted, segment, num_segments=slots_out + 1)]
    all_gather x3 -> x0, blocking collectives: 42.4 us -> none  [the longest x1 24.9 us: shards(): b_tags_all = lax.all_gather(b_tags, 'row', axis=1, tiled=True)]
    reshape x1, local copies, waits for them, and re-layouts: 24.7 us -> 0.08 us  [line(): flat = values.reshape(-1).astype(F32)]
    dot_general x1 -> x0, matrix products: 14.8 us -> none  [shards(): jnp.einsum('aij,atjk->atik', a_all, chosen, preferred_element_type=jnp.fl...]
    gather x4 -> x0, local copies, waits for them, and re-layouts: 12.7 us -> none  [the longest x1 11.5 us: shards(): chosen = b_all[needed]]
  transfers between devices with their start and end apart: 3 -> 0, of which waited for: 3 -> 0; matrix products, arithmetic and copies ran while one was open for 5% -> 0% of each run, Pallas kernels for 0% -> 0%
where the time goes in v1:
time: 193 us; the launch traced here: 192 us
  Pallas kernels  182 us (94%)
  local copies, waits for them, and re-layouts  5.43 us (3%)
  other arithmetic  4.67 us (2%)
    pallas_call x1, Pallas kernels, shards(): pl.pallas_call(functools.partial(kernel, dims), out_shape=jax.ShapeDtypeS...  182 us
    unnamed x2, local copies, waits for them, and re-layouts  3.98 us

profile of v1, /device:TPU:1, one launch (start us, length us, event | category | flops | bytes accessed | tf_op | source)
XLA Modules:
  0.0 192.4 jit_solution(4365202952167516641)
XLA Ops:
  0.0 0.7 pad_bitcast_fusion.6
  0.7 0.7 convert_element_type.30
  1.3 0.7 convert_element_type.31
  2.0 0.5 broadcast.20
  2.5 1.3 reduce.7
  3.8 0.1 reshape.9
  3.9 0.7 convert_element_type.34
  4.6 0.7 convert_element_type.35
  5.2 0.7 convert_reduce_fusion
  5.9 0.1 convert_element_type.33
  6.0 0.6 stack.32.meta
  6.6 182.3 %shard_map.91 = bf16[20,256,256]{2,1,0:T(8,128)(2,1)} custom-call(bf16[8,256,256]{2,1,0:T(8,128)(2,1)} %a_hbm.1, bf16[2,3,256,256]{3,2,1,0:T(8,128)(2,1)} %bitcast.15, f32[8,128]{1,0:T(8,128)} %stack.32.meta), custom_call_target="tpu_custom_call" | custom-call | tf_op jit(solution)/shard_map/pallas_call | solution.py:389
  188.9 3.5 %copy.11 = bf16[20,256,256]{2,1,0:T(8,128)(2,1)} copy(bf16[20,256,256]{2,1,0:T(8,128)(2,1)} %shard_map.91) | data formatting | bytes 5242880
  (3 shorter events, 0.0 us)

commit v2 on v0

v2 whole, which is shorter than its diff:
```python
import functools

import jax
import jax.numpy as jnp
from jax import lax
from jax.experimental import pallas as pl
from jax.experimental.pallas import tpu as pltpu
from jax.sharding import PartitionSpec as P

MESH = pl.DeviceIdType.MESH
LANES = 128
ROW_KEY = 1024.0
F32 = jnp.float32


def iota(shape, dim):
    return lax.broadcasted_iota(jnp.int32, shape, dim)


def schedule(dims, meta_x, meta_y, meta_z, tab_int, tab_scale):
    n_x, n_y, n_r, a_cap, per, kb, c_cap = dims
    n_c = n_y * a_cap
    n_a = 2 * n_c
    n_g = n_r * per
    eye = iota((a_cap, LANES), 0) == iota((a_cap, LANES), 1)
    lane = iota((n_c, LANES), 1)
    slots, weights, a_ids, b_ids = [], [], [], []
    n_slots = n_x * c_cap
    for kind in range(2):

        def column(which):
            parts = [
                jnp.sum(jnp.where(eye, meta_y[kind, c, which : which + 1, :], 0.0), axis=1, keepdims=True)
                for c in range(n_y)
            ]
            return jnp.concatenate(parts, axis=0)

        a_scale, a_rows, a_cols = column(0), column(1), column(2)
        group = a_cols.astype(jnp.int32) // n_x
        b_scale = jnp.zeros((n_c, LANES), F32)
        b_cols = jnp.zeros((n_c, LANES), F32)
        for g in range(n_g):
            here = group == g
            d, inner = g // per, g % per
            b_scale = jnp.where(here, meta_z[kind, d, 3 + inner : 4 + inner, :], b_scale)
            b_cols = jnp.where(here, meta_z[kind, d, 5 + inner : 6 + inner, :], b_cols)
        for t in range(kb):
            col = jnp.sum(jnp.where(lane == t, b_cols, 0.0), axis=1, keepdims=True)
            scale = jnp.sum(jnp.where(lane == t, b_scale, 0.0), axis=1, keepdims=True)
            key = a_rows * ROW_KEY + col
            found = jnp.zeros((n_c, LANES), F32)
            for e in range(n_x):
                hit = (key == meta_x[e, 7:8, :]) & (lane < c_cap)
                found = jnp.where(hit, (lane + (e * c_cap + 1)).astype(F32), found)
            slot = jnp.max(found, axis=1, keepdims=True)
            slots.append(jnp.where(slot > 0, slot - 1, float(n_slots)))
            weights.append(a_scale * scale)
            a_ids.append((iota((n_c, 1), 0) + kind * n_c).astype(F32))
            b_ids.append(((group + kind * n_g) * kb + t).astype(F32))
    slot = jnp.concatenate(slots, axis=0)
    weight = jnp.concatenate(weights, axis=0)
    a_id = jnp.concatenate(a_ids, axis=0)
    b_id = jnp.concatenate(b_ids, axis=0)
    n_p = kb * n_a
    width = tab_int.shape[1]
    place, lane = iota((n_p, width), 0), iota((n_p, width), 1)
    row_slot = jnp.sum(jnp.where(place == lane, slot, 0.0), axis=0, keepdims=True)
    row_slot = jnp.where(lane[:1] < n_p, row_slot, 1e6)
    earlier = (row_slot == slot) & (lane < place)
    before = (row_slot < slot) | earlier
    rank = jnp.sum(jnp.where(before, 1.0, 0.0), axis=1, keepdims=True)
    keep = jnp.where(jnp.sum(jnp.where(earlier, 1.0, 0.0), axis=1, keepdims=True) > 0, 1.0, 0.0)
    lane_f = lane.astype(F32)
    mine = rank == lane_f

    def ordered(values):
        return jnp.sum(jnp.where(mine, values, 0.0), axis=0, keepdims=True)

    last = jnp.sum(jnp.where(slot <= lane_f, 1.0, 0.0), axis=0, keepdims=True) - 1.0
    some = jnp.sum(jnp.where(slot == lane_f, 1.0, 0.0), axis=0, keepdims=True)
    last = jnp.where(some > 0, last, float(n_p))
    zero = jnp.zeros((1, width), F32)
    table = jnp.concatenate(
        [ordered(a_id), ordered(b_id), last, zero, zero, zero, zero, zero], axis=0
    ).astype(jnp.int32)
    which = iota(table.shape, 0)
    top = jnp.where(which == 0, n_a - 1, jnp.where(which == 1, 2 * n_g * kb - 1, n_p))
    tab_int[...] = jnp.clip(table, 0, top)
    tab_scale[...] = jnp.concatenate(
        [ordered(weight), ordered(keep), zero, zero, zero, zero, zero, zero], axis=0
    )


def kernel(
    dims, a_hbm, b_hbm, a_scale, a_rows, a_cols, b_scale, b_cols, c_rows, c_cols, out_hbm,
    a_all, b_all, meta, meta_x, meta_y, meta_z, tab_int, tab_scale, ids, scales,
    acc, prod, to_mirror, from_mirror, to_pair, result,
    local_sem, meta_send, meta_recv, ring_send, ring_recv, core_send, core_recv, raw_send, raw_recv, a_send, a_recv,
    m_send, m_recv, p_send, p_recv, out_sem,
):
    n_x, n_y, n_r, a_cap, per, kb, c_cap = dims
    n_z = n_r // 2
    n_g = n_r * per
    n_c = n_y * a_cap
    half = result.shape[2]
    row, col, dep = lax.axis_index("row"), lax.axis_index("col"), lax.axis_index("depth")
    z, core = row // 2, row % 2

    def at_z(step):
        return (lax.rem(z + step + n_z, n_z) * 2 + core, col, dep)

    def at_y(step):
        return (row, lax.rem(col + step + n_y, n_y), dep)

    def at_x(step):
        return (row, col, lax.rem(dep + step + n_x, n_x))

    sibling = (z * 2 + 1 - core, col, dep)
    d_pair, d_mirror, d_far = dep + 1 - 2 * (dep % 2), n_x - 1 - dep, lax.rem(dep + 2, n_x)
    pair, mirror = (row, col, d_pair), (row, col, d_mirror)
    side = ((dep + 1) // 2) % 2
    my_cols = pl.ds(pl.multiple_of(side * half, half), half)
    pair_cols = pl.ds(pl.multiple_of((1 - side) * half, half), half)

    meta[...] = jnp.zeros_like(meta)
    meta[0:1, 0:a_cap] = a_scale[...]
    meta[1:2, 0:a_cap] = a_rows[...].astype(F32)
    meta[2:3, 0:a_cap] = a_cols[...].astype(F32)
    meta[3 : 3 + per, 0:kb] = b_scale[...]
    meta[5 : 5 + per, 0:kb] = b_cols[...].astype(F32)
    meta[7:8, 0:c_cap] = c_rows[...].astype(F32) * ROW_KEY + c_cols[...].astype(F32)

    barrier = pltpu.get_barrier_semaphore()
    partners = [sibling, at_z(1), at_z(-1)] + [at_y(j) for j in range(1, n_y)] + [at_x(j) for j in range(1, n_x)]
    for partner in partners:
        pl.semaphore_signal(barrier, inc=1, device_id=partner, device_id_type=MESH)
    pl.semaphore_wait(barrier, len(partners))

    sends = []

    def copy(src, dst, send, recv, device):
        return pltpu.make_async_remote_copy(
            src_ref=src, dst_ref=dst, send_sem=send, recv_sem=recv, device_id=device, device_id_type=MESH
        )

    def push(src, dst, send, recv, device):
        made = copy(src, dst, send, recv, device)
        made.start()
        sends.append(made)

    def pulled(dst, send, recv):
        copy(dst, dst, send, recv, sibling).wait_recv()

    count = 0
    meta_waits = []
    for j in range(1, n_y):
        push(meta, meta_y.at[0, col], meta_send.at[count], meta_recv.at[count], at_y(j))
        meta_waits.append((meta_y.at[0, lax.rem(col - j + n_y, n_y)], count))
        count += 1
    for j in range(1, n_x):
        push(meta, meta_x.at[dep], meta_send.at[count], meta_recv.at[count], at_x(j))
        meta_waits.append((meta_x.at[lax.rem(dep - j + n_x, n_x)], count))
        count += 1
    push(meta, meta_z.at[0, row], meta_send.at[count], meta_recv.at[count], sibling)
    meta_waits.append((meta_z.at[0, z * 2 + 1 - core], count))
    count += 1
    hops_up, hops_down = n_z // 2, (n_z - 1) // 2
    ring_meta = count
    push(meta, meta_z.at[0, row], meta_send.at[count], meta_recv.at[count], at_z(1))
    push(meta, meta_z.at[0, row], meta_send.at[count + 1], meta_recv.at[count + 1], at_z(-1))
    count += 2 * hops_up
    core_meta = count
    count += 2 * hops_up
    pair_meta = count

    up, down = at_z(1), at_z(-1)
    units = [(kind, inner) for kind in range(2) for inner in range(per)]
    n_u = len(units)

    def b_unit(origin_z, origin_core, unit):
        kind, inner = units[unit]
        return b_all.at[pl.ds(((kind * n_r + origin_z * 2 + origin_core) * per + inner) * kb, kb)]

    def a_part(kind, origin, first, size):
        return a_all.at[pl.ds((kind * n_y + origin) * a_cap + first, size)]

    def ring_slot(direction, step, unit):
        return (direction * hops_up + step) * n_u + unit

    def hops(direction, unit):
        return hops_up if units[unit][0] == direction else hops_down

    def send_first(src, unit):
        for direction, device in ((0, up), (1, down)):
            index = ring_slot(direction, 0, unit)
            push(src, b_unit(z, core, unit), ring_send.at[index], ring_recv.at[index], device)
        push(src, b_unit(z, core, unit), core_send.at[unit], core_recv.at[unit], sibling)

    for inner in range(per):
        push(b_hbm.at[inner, :, :, pair_cols], b_unit(z, core, per + inner), raw_send.at[inner], raw_recv.at[inner], pair)
        send_first(b_hbm.at[inner, :, :, my_cols], inner)

    mid = a_cap // 2
    n_ring = a_cap * 3 // 4
    n_part = n_ring // 2
    y_up, y_down = at_y(1), at_y(-1)
    left, right, across = at_y(-1)[1], at_y(1)[1], at_y(2)[1]

    def own_a(first, size, slot, device):
        push(a_hbm.at[pl.ds(first, size)], a_part(0, col, first, size), a_send.at[slot], a_recv.at[slot], device)

    own_a(0, mid, 0, y_up)
    own_a(mid, mid, 3, y_down)

    def raw_a(first, size, slot):
        push(a_hbm.at[pl.ds(first, size)], a_part(1, col, first, size), a_send.at[slot], a_recv.at[slot], pair)

    raw_a(0, n_part, 12)
    own_a(mid, mid, 1, y_up)
    own_a(0, mid, 4, y_down)
    raw_a(n_part, n_part, 13)
    raw_a(n_ring, a_cap - n_ring, 14)
    local = [
        pltpu.make_async_copy(a_hbm, a_part(0, col, 0, a_cap), local_sem.at[0]),
    ]
    for inner in range(per):
        local.append(
            pltpu.make_async_copy(b_hbm.at[inner, :, :, my_cols], b_unit(z, core, inner), local_sem.at[1 + inner])
        )
    for made in local:
        made.start()
    meta_x[dep] = meta[...]
    meta_y[0, col] = meta[...]
    meta_z[0, row] = meta[...]

    def forward_meta(step):
        for direction, limit in ((0, hops_up), (1, hops_down)):
            if step >= limit:
                continue
            origin_z = lax.rem(z - step - 1 + n_z, n_z) if direction == 0 else lax.rem(z + step + 1, n_z)
            here = meta_z.at[0, origin_z * 2 + core]
            index = ring_meta + 2 * step + direction
            pulled(here, meta_send.at[index], meta_recv.at[index])
            if step + 1 < limit:
                push(here, here, meta_send.at[index + 2], meta_recv.at[index + 2], up if direction == 0 else down)
            index = core_meta + 2 * step + direction
            push(here, here, meta_send.at[index], meta_recv.at[index], sibling)
            meta_waits.append((meta_z.at[0, origin_z * 2 + 1 - core], index))

    def pair_tables():
        for here, index in meta_waits:
            pulled(here, meta_send.at[index], meta_recv.at[index])
        push(meta_y.at[0], meta_y.at[1], meta_send.at[pair_meta], meta_recv.at[pair_meta], pair)
        push(meta_z.at[0], meta_z.at[1], meta_send.at[pair_meta + 1], meta_recv.at[pair_meta + 1], pair)

    core_waits = [(b_unit(z, 1 - core, unit), unit) for unit in range(n_u)]

    def forward_raw(inner):
        here = b_unit(z, core, per + inner)
        pulled(here, raw_send.at[inner], raw_recv.at[inner])
        send_first(here, per + inner)

    def forward_b(step, unit):
        for direction in range(2):
            limit = hops(direction, unit)
            if step >= limit:
                continue
            origin_z = lax.rem(z - step - 1 + n_z, n_z) if direction == 0 else lax.rem(z + step + 1, n_z)
            here = b_unit(origin_z, core, unit)
            index = ring_slot(direction, step, unit)
            pulled(here, ring_send.at[index], ring_recv.at[index])
            if step + 1 < limit:
                index = ring_slot(direction, step + 1, unit)
                push(here, here, ring_send.at[index], ring_recv.at[index], up if direction == 0 else down)
            index = n_u + ring_slot(direction, step, unit)
            push(here, here, core_send.at[index], core_recv.at[index], sibling)
            core_waits.append((b_unit(origin_z, 1 - core, unit), index))

    def arrived(kind, origin, first, size, slot):
        here = a_part(kind, origin, first, size)
        pulled(here, a_send.at[slot], a_recv.at[slot])
        return here

    def hand_on(here, slot, device):
        push(here, here, a_send.at[slot], a_recv.at[slot], device)

    def to_pair_a(origin, slot):
        size = a_cap - n_ring
        push(a_part(0, origin, n_ring, size), a_part(1, origin, n_ring, size), a_send.at[slot], a_recv.at[slot], pair)

    forward_meta(0)
    forward_raw(0)
    forward_b(0, 0)
    forward_raw(1)
    forward_b(0, 1)
    forward_meta(1)
    hand_on(arrived(0, left, 0, mid, 0), 2, y_up)
    hand_on(arrived(0, right, mid, mid, 3), 5, y_down)
    to_pair_a(right, 16)
    forward_b(0, 2)
    forward_meta(2)
    here = arrived(1, col, 0, n_part, 12)
    hand_on(here, 6, y_up)
    hand_on(here, 10, y_down)
    forward_b(0, 3)
    forward_meta(3)
    forward_b(1, 0)
    arrived(0, left, mid, mid, 1)
    to_pair_a(left, 15)
    here = arrived(1, col, n_part, n_part, 13)
    hand_on(here, 7, y_up)
    hand_on(here, 9, y_down)
    forward_b(1, 1)
    pair_tables()
    forward_b(1, 2)
    arrived(0, across, mid, mid, 5)
    to_pair_a(across, 17)
    forward_b(1, 3)
    forward_b(2, 0)
    hand_on(arrived(1, left, 0, n_part, 6), 8, y_up)
    forward_b(2, 1)
    hand_on(arrived(1, right, n_part, n_part, 9), 11, y_down)
    forward_b(2, 2)
    pulled(meta_y.at[1], meta_send.at[pair_meta], meta_recv.at[pair_meta])
    pulled(meta_z.at[1], meta_send.at[pair_meta + 1], meta_recv.at[pair_meta + 1])
    schedule(dims, meta_x, meta_y, meta_z, tab_int, tab_scale)
    table = [
        pltpu.make_async_copy(tab_int, ids, local_sem.at[3]),
        pltpu.make_async_copy(tab_scale, scales, local_sem.at[4]),
    ]
    for made in table:
        made.start()
    forward_b(2, 3)
    for unit in range(n_u):
        forward_b(3, unit)
    for made in table + local:
        made.wait()
    arrived(0, right, 0, mid, 4)
    arrived(0, across, 0, mid, 2)
    arrived(1, col, n_ring, a_cap - n_ring, 14)
    arrived(1, left, n_part, n_part, 7)
    arrived(1, right, 0, n_part, 10)
    arrived(1, across, 0, n_part, 8)
    arrived(1, across, n_part, n_part, 11)
    arrived(1, left, n_ring, a_cap - n_ring, 15)
    arrived(1, right, n_ring, a_cap - n_ring, 16)
    arrived(1, across, n_ring, a_cap - n_ring, 17)
    for here, index in core_waits:
        pulled(here, core_send.at[index], core_recv.at[index])

    n_p = kb * 2 * n_c
    acc[...] = jnp.zeros_like(acc)
    prod[n_p] = jnp.zeros(prod.shape[1:], prod.dtype)

    def bounded(index, size):
        return jnp.clip(index, 0, size - 1)

    @pl.loop(0, n_p, unroll=8)
    def _(j):
        left_block = a_all[bounded(ids[0, j], 2 * n_c)]
        right_block = b_all[bounded(ids[1, j], 2 * n_g * kb)]
        product = jnp.dot(left_block, right_block, preferred_element_type=F32)
        total = acc[...] * scales[1, j] + product * scales[0, j]
        acc[...] = total
        prod[j] = total.astype(prod.dtype)

    piece = 4
    steps = c_cap // piece

    def own(dest, index):
        return prod[bounded(ids[2, dest * c_cap + index], n_p + 1)]

    def part(refs, stage, k):
        return refs.at[pl.ds(stage * c_cap + k * piece, piece)]

    def send_mirror(stage, k):
        index = stage * steps + k
        return copy(part(to_mirror, stage, k), part(from_mirror, stage, k), m_send.at[index], m_recv.at[index], mirror)

    def send_pair(k):
        there = out_hbm.at[pl.ds(k * piece, piece), :, my_cols]
        return copy(part(to_pair, 0, k), there, p_send.at[k], p_recv.at[k], pair)

    def write(k):
        return pltpu.make_async_copy(part(result, 0, k), out_hbm.at[pl.ds(k * piece, piece), :, my_cols], out_sem.at[k])

    for stage, dest in ((0, d_far), (1, d_mirror)):

        @pl.loop(0, steps)
        def _(k):
            for i in range(piece):
                to_mirror[stage * c_cap + k * piece + i] = own(dest, k * piece + i)
            send_mirror(stage, k).start()

    def add(dest, stage, m):
        return (own(dest, m).astype(F32) + from_mirror[stage * c_cap + m].astype(F32)).astype(prod.dtype)

    @pl.loop(0, steps)
    def _(k):
        send_mirror(0, k).wait_recv()
        for i in range(piece):
            to_pair[k * piece + i] = add(d_pair, 0, k * piece + i)
        send_pair(k).start()

    @pl.loop(0, steps)
    def _(k):
        send_mirror(1, k).wait_recv()
        for i in range(piece):
            result[k * piece + i] = add(dep, 1, k * piece + i)
        write(k).start()

    @pl.loop(0, steps)
    def _(k):
        write(k).wait()
        here = out_hbm.at[pl.ds(k * piece, piece), :, pair_cols]
        copy(here, here, p_send.at[k], p_recv.at[k], pair).wait_recv()
        send_pair(k).wait_send()
        send_mirror(0, k).wait_send()
        send_mirror(1, k).wait_send()

    for made in sends:
        made.wait_send()


def shards(a_blocks, a_scale, a_rows, a_cols, b_blocks, b_scale, b_cols, c_rows, c_cols):
    edge = a_blocks.shape[1]
    half = edge // 2
    a_cap, c_cap = a_blocks.shape[0], c_rows.shape[0]
    per, kb = b_blocks.shape[0], b_blocks.shape[3]
    n_r, n_y, n_x = lax.axis_size("row"), lax.axis_size("col"), lax.axis_size("depth")
    dims = (n_x, n_y, n_r, a_cap, per, kb, c_cap)
    n_p = kb * n_y * a_cap * 2
    width = -(-n_p // LANES) * LANES
    dtype = a_blocks.dtype
    block, part = (edge, edge), (edge, half)
    dma = pltpu.SemaphoreType.DMA
    hops = n_r // 4
    n_meta = (n_y - 1) + (n_x - 1) + 1 + 4 * hops + 2
    n_ring = 2 * hops * 2 * per
    any_space = pl.BlockSpec(memory_space=pl.ANY)
    vmem = pl.BlockSpec(memory_space=pltpu.VMEM)
    return pl.pallas_call(
        functools.partial(kernel, dims),
        out_shape=jax.ShapeDtypeStruct((c_cap,) + block, dtype),
        in_specs=[any_space, any_space] + [vmem] * 7,
        out_specs=any_space,
        scratch_shapes=[
            pltpu.VMEM((2 * n_y * a_cap,) + block, dtype),
            pltpu.VMEM((2 * n_r * per * kb,) + part, dtype),
            pltpu.VMEM((8, LANES), F32),
            pltpu.VMEM((n_x, 8, LANES), F32),
            pltpu.VMEM((2, n_y, 8, LANES), F32),
            pltpu.VMEM((2, n_r, 8, LANES), F32),
            pltpu.VMEM((8, width), jnp.int32),
            pltpu.VMEM((8, width), F32),
            pltpu.SMEM((8, width), jnp.int32),
            pltpu.SMEM((8, width), F32),
            pltpu.VMEM(part, F32),
            pltpu.VMEM((n_p + 1,) + part, dtype),
            pltpu.VMEM((2 * c_cap,) + part, dtype),
            pltpu.VMEM((2 * c_cap,) + part, dtype),
            pltpu.VMEM((c_cap,) + part, dtype),
            pltpu.VMEM((c_cap,) + part, dtype),
            dma((5,)),
            dma((n_meta,)),
            dma((n_meta,)),
            dma((n_ring,)),
            dma((n_ring,)),
            dma((2 * per + n_ring,)),
            dma((2 * per + n_ring,)),
            dma((per,)),
            dma((per,)),
            dma((18,)),
            dma((18,)),
            dma((2 * c_cap,)),
            dma((2 * c_cap,)),
            dma((c_cap,)),
            dma((c_cap,)),
            dma((c_cap,)),
        ],
        compiler_params=pltpu.CompilerParams(
            collective_id=0, has_side_effects=True, vmem_limit_bytes=60 * 1024 * 1024
        ),
    )(
        a_blocks,
        b_blocks.reshape(per, kb, edge, edge),
        a_scale.reshape(1, a_cap),
        a_rows.reshape(1, a_cap),
        a_cols.reshape(1, a_cap),
        b_scale.reshape(per, kb),
        b_cols.reshape(per, kb),
        c_rows.reshape(1, c_cap),
        c_cols.reshape(1, c_cap),
    )


def solution(mesh):
    return jax.shard_map(
        shards,
        mesh=mesh,
        in_specs=(
            P(("row", "col", "depth"), None, None),
            P(("row", "col", "depth")),
            P(("row", "col", "depth")),
            P(("row", "col", "depth")),
            P("row", "col", "depth", None, None, None),
            P("row", "col", "depth", None),
            P("row", "col", "depth", None),
            P(("row", "col", "depth")),
            P(("row", "col", "depth")),
        ),
        out_specs=P(("row", "col", "depth"), None, None),
        check_vma=False,
    )
```

time: 363 us -> 150 us (0.41)
  waiting for transfers between devices: 175 us -> 0 us
  Pallas kernels: 0 us -> 146 us
  other arithmetic: 57.6 us -> 0 us
  local copies, waits for them, and re-layouts: 59.6 us -> 3.47 us
  blocking collectives: 42.4 us -> 0 us
  matrix products: 14.8 us -> 0 us
  between operations: 13.1 us -> 0.01 us
    pallas_call x0 -> x1, Pallas kernels: none -> 146 us  [shards(): pl.pallas_call(functools.partial(kernel, dims), out_shape=jax.ShapeDtypeS...]
    reduce_scatter x1 -> x0, waiting for transfers between devices: 101 us -> none  [shards(): lax.psum_scatter(partial_sums.astype(jnp.bfloat16), 'depth', scatter_dime...]
    all_gather x2 -> x0, waiting for transfers between devices: 72 us -> none  [the longest x1 39.3 us: shards(): a_all = lax.all_gather(a_blocks, 'col', axis=0, tiled=True)]
    scatter-add x1 -> x0, other arithmetic: 53.1 us -> none  [shards(): jax.ops.segment_sum(weighted, segment, num_segments=slots_out + 1)]
    all_gather x3 -> x0, blocking collectives: 42.4 us -> none  [the longest x1 24.9 us: shards(): b_tags_all = lax.all_gather(b_tags, 'row', axis=1, tiled=True)]
    reshape x1 -> x0, local copies, waits for them, and re-layouts: 24.7 us -> none  [shards(): (products * weights[:, :, None, None]).reshape(-1, block_edge, block_edge)]
    dot_general x1 -> x0, matrix products: 14.8 us -> none  [shards(): jnp.einsum('aij,atjk->atik', a_all, chosen, preferred_element_type=jnp.fl...]
    gather x4 -> x0, local copies, waits for them, and re-layouts: 12.7 us -> none  [the longest x1 11.5 us: shards(): chosen = b_all[needed]]
  transfers between devices with their start and end apart: 3 -> 0, of which waited for: 3 -> 0; matrix products, arithmetic and copies ran while one was open for 5% -> 0% of each run, Pallas kernels for 0% -> 0%
where the time goes in v2:
time: 150 us
  Pallas kernels  146 us (97%)
  local copies, waits for them, and re-layouts  3.47 us (2%)
    pallas_call x1, Pallas kernels, shards(): pl.pallas_call(functools.partial(kernel, dims), out_shape=jax.ShapeDtypeS...  146 us
    unnamed x1, local copies, waits for them, and re-layouts  3.47 us

profile of v2, /device:TPU:1, one launch (start us, length us, event | category | flops | bytes accessed | tf_op | source)
XLA Modules:
  0.0 149.7 jit_solution(18196140614242912889)
XLA Ops:
  0.0 146.2 %shard_map.91 = bf16[20,256,256]{2,1,0:T(8,128)(2,1)} custom-call(bf16[8,256,256]{2,1,0:T(8,128)(2,1)} %a_hbm.1, bf16[2,3,256,256]{3,2,1,0:T(8,128)(2,1)} %bitcast.8, f32[1,8]{1,0:T(1,128)} %bitcast.11, s32[1,8]{1,0:T(1,128)} %bitcast.12, s32[1,8]{1,0:T(1,128)} %bitcast.13, f32[2,3]{1,0:T(2,128)} %bitcast.9, s32[2,3]{1,0:T(2,128)} %bitcast.10, ...), custom_call_target="tpu_custom_call" | custom-call | tf_op jit(solution)/shard_map/pallas_call | solution.py:442
  146.2 3.5 %copy.11 = bf16[20,256,256]{2,1,0:T(8,128)(2,1)} copy(bf16[20,256,256]{2,1,0:T(8,128)(2,1)} %shard_map.91) | data formatting | bytes 5242880

commit v3 on v2

v3 whole, which is shorter than its diff:
```python
import functools

import jax
import jax.numpy as jnp
from jax import lax
from jax.experimental import pallas as pl
from jax.experimental.pallas import tpu as pltpu
from jax.sharding import PartitionSpec as P

MESH = pl.DeviceIdType.MESH
LANES = 128
ROW_KEY = 1024.0
F32 = jnp.float32


def iota(shape, dim):
    return lax.broadcasted_iota(jnp.int32, shape, dim)


def schedule(dims, kind, meta_x, meta_y, meta_z, tab_int, tab_scale):
    n_x, n_y, n_r, a_cap, per, kb, c_cap = dims
    n_a = n_y * a_cap
    n_g = n_r * per
    n_slots = n_x * c_cap
    eye = iota((a_cap, LANES), 0) == iota((a_cap, LANES), 1)
    lane = iota((n_a, LANES), 1)

    def column(which):
        parts = [
            jnp.sum(jnp.where(eye, meta_y[kind, c, which : which + 1, :], 0.0), axis=1, keepdims=True)
            for c in range(n_y)
        ]
        return jnp.concatenate(parts, axis=0)

    a_scale, a_rows, a_cols = column(0), column(1), column(2)
    group = a_cols.astype(jnp.int32) // n_x
    b_scale = jnp.zeros((n_a, LANES), F32)
    b_cols = jnp.zeros((n_a, LANES), F32)
    for g in range(n_g):
        here = group == g
        d, inner = g // per, g % per
        b_scale = jnp.where(here, meta_z[kind, d, 3 + inner : 4 + inner, :], b_scale)
        b_cols = jnp.where(here, meta_z[kind, d, 5 + inner : 6 + inner, :], b_cols)
    slots, weights, b_ids = [], [], []
    for t in range(kb):
        col = jnp.sum(jnp.where(lane == t, b_cols, 0.0), axis=1, keepdims=True)
        scale = jnp.sum(jnp.where(lane == t, b_scale, 0.0), axis=1, keepdims=True)
        key = a_rows * ROW_KEY + col
        found = jnp.zeros((n_a, LANES), F32)
        for e in range(n_x):
            hit = (key == meta_x[e, 7:8, :]) & (lane < c_cap)
            found = jnp.where(hit, (lane + (e * c_cap + 1)).astype(F32), found)
        slot = jnp.max(found, axis=1, keepdims=True)
        slots.append(jnp.where(slot > 0, slot - 1, float(n_slots)))
        weights.append(a_scale * scale)
        b_ids.append((group * kb + t).astype(F32))
    slot, weight = jnp.concatenate(slots, axis=0), jnp.concatenate(weights, axis=0)
    a_id = jnp.concatenate([iota((n_a, 1), 0).astype(F32)] * kb, axis=0)
    b_id = jnp.concatenate(b_ids, axis=0)
    n_p = kb * n_a
    width = tab_int.shape[1]
    place, lane = iota((n_p, width), 0), iota((n_p, width), 1)
    row_slot = jnp.sum(jnp.where(place == lane, slot, 0.0), axis=0, keepdims=True)
    row_slot = jnp.where(lane[:1] < n_p, row_slot, 1e6)
    earlier = (row_slot == slot) & (lane < place)
    before = (row_slot < slot) | earlier
    rank = jnp.sum(jnp.where(before, 1.0, 0.0), axis=1, keepdims=True)
    keep = jnp.where(jnp.sum(jnp.where(earlier, 1.0, 0.0), axis=1, keepdims=True) > 0, 1.0, 0.0)
    lane_f = lane.astype(F32)
    mine = rank == lane_f

    def ordered(values):
        return jnp.sum(jnp.where(mine, values, 0.0), axis=0, keepdims=True)

    last = jnp.sum(jnp.where(slot <= lane_f, 1.0, 0.0), axis=0, keepdims=True) - 1.0
    some = jnp.sum(jnp.where(slot == lane_f, 1.0, 0.0), axis=0, keepdims=True)
    last = jnp.where(some > 0, last, float(n_p))
    zero = jnp.zeros((1, width), F32)
    table = jnp.concatenate(
        [ordered(a_id), ordered(b_id), last, zero, zero, zero, zero, zero], axis=0
    ).astype(jnp.int32)
    which = iota(table.shape, 0)
    top = jnp.where(which == 0, n_a - 1, jnp.where(which == 1, n_g * kb - 1, n_p))
    tab_int[...] = jnp.clip(table, 0, top)
    tab_scale[...] = jnp.concatenate(
        [ordered(weight), ordered(keep), zero, zero, zero, zero, zero, zero], axis=0
    )


def kernel(
    dims, a_hbm, b_hbm, a_scale, a_rows, a_cols, b_scale, b_cols, c_rows, c_cols, out_hbm,
    a_own, a_pair, b_first, b_second, raw_own, raw_pair, meta, meta_x, meta_y, meta_z,
    tab_int1, tab_scale1, ids1, scales1, tab_int2, tab_scale2, ids2, scales2,
    acc, prod1, prod2, prod3, to_right, to_left, from_left, from_right, to_mirror, from_mirror, to_pair, from_pair,
    result,
    local_sem, meta_send, meta_recv, ring_send, ring_recv, core_send, core_recv, raw_send, raw_recv, a_send, a_recv,
    r_send, r_recv, l_send, l_recv, m_send, m_recv, p_send, p_recv, out_sem,
):
    n_x, n_y, n_r, a_cap, per, kb, c_cap = dims
    n_z = n_r // 2
    n_g = n_r * per
    n_c = n_y * a_cap
    half = b_first.shape[2]
    quarter = half // 2
    row, col, dep = lax.axis_index("row"), lax.axis_index("col"), lax.axis_index("depth")
    z, core = row // 2, row % 2

    def at_z(step):
        return (lax.rem(z + step + n_z, n_z) * 2 + core, col, dep)

    def at_y(step):
        return (row, lax.rem(col + step + n_y, n_y), dep)

    def at_x(step):
        return (row, col, lax.rem(dep + step + n_x, n_x))

    sibling = (z * 2 + 1 - core, col, dep)
    d_pair, d_mirror, d_far = dep + 1 - 2 * (dep % 2), n_x - 1 - dep, lax.rem(dep + 2, n_x)
    pair, mirror = (row, col, d_pair), (row, col, d_mirror)
    side = ((dep + 1) // 2) % 2
    first_cols, second_cols = pl.ds(0, half), pl.ds(half, half)
    low_lanes = iota((1, half), 1) < quarter

    meta[...] = jnp.zeros_like(meta)
    meta[0:1, 0:a_cap] = a_scale[...]
    meta[1:2, 0:a_cap] = a_rows[...].astype(F32)
    meta[2:3, 0:a_cap] = a_cols[...].astype(F32)
    meta[3 : 3 + per, 0:kb] = b_scale[...]
    meta[5 : 5 + per, 0:kb] = b_cols[...].astype(F32)
    meta[7:8, 0:c_cap] = c_rows[...].astype(F32) * ROW_KEY + c_cols[...].astype(F32)

    barrier = pltpu.get_barrier_semaphore()
    partners = [sibling, at_z(1), at_z(-1)] + [at_y(j) for j in range(1, n_y)] + [at_x(j) for j in range(1, n_x)]
    for partner in partners:
        pl.semaphore_signal(barrier, inc=1, device_id=partner, device_id_type=MESH)
    pl.semaphore_wait(barrier, len(partners))

    sends = []

    def copy(src, dst, send, recv, device):
        return pltpu.make_async_remote_copy(
            src_ref=src, dst_ref=dst, send_sem=send, recv_sem=recv, device_id=device, device_id_type=MESH
        )

    def push(src, dst, send, recv, device):
        made = copy(src, dst, send, recv, device)
        made.start()
        sends.append(made)

    def pulled(dst, send, recv):
        copy(dst, dst, send, recv, sibling).wait_recv()

    count = 0
    meta_waits = []
    for j in range(1, n_y):
        push(meta, meta_y.at[0, col], meta_send.at[count], meta_recv.at[count], at_y(j))
        meta_waits.append((meta_y.at[0, lax.rem(col - j + n_y, n_y)], count))
        count += 1
    for j in range(1, n_x):
        push(meta, meta_x.at[dep], meta_send.at[count], meta_recv.at[count], at_x(j))
        meta_waits.append((meta_x.at[lax.rem(dep - j + n_x, n_x)], count))
        count += 1
    push(meta, meta_z.at[0, row], meta_send.at[count], meta_recv.at[count], sibling)
    meta_waits.append((meta_z.at[0, z * 2 + 1 - core], count))
    count += 1
    hops_up, hops_down = n_z // 2, (n_z - 1) // 2
    ring_meta = count
    push(meta, meta_z.at[0, row], meta_send.at[count], meta_recv.at[count], at_z(1))
    push(meta, meta_z.at[0, row], meta_send.at[count + 1], meta_recv.at[count + 1], at_z(-1))
    count += 2 * hops_up
    core_meta = count
    count += 2 * hops_up
    pair_meta = count

    up, down = at_z(1), at_z(-1)
    units = [(kind, inner) for kind in range(2) for inner in range(per)]
    n_u = len(units)

    def b_unit(origin_z, origin_core, unit):
        kind, inner = units[unit]
        refs = b_second if kind else b_first
        return refs.at[pl.ds(((origin_z * 2 + origin_core) * per + inner) * kb, kb)]

    def a_part(kind, origin, first):
        refs = a_pair if kind else a_own
        return refs.at[pl.ds(origin * a_cap + first, a_cap // 2)]

    def ring_slot(direction, step, unit):
        return (direction * hops_up + step) * n_u + unit

    def hops(direction, unit):
        return hops_up if units[unit][1] == direction else hops_down

    def send_first(src, unit):
        for direction, device in ((0, up), (1, down)):
            index = ring_slot(direction, 0, unit)
            push(src, b_unit(z, core, unit), ring_send.at[index], ring_recv.at[index], device)
        push(src, b_unit(z, core, unit), core_send.at[unit], core_recv.at[unit], sibling)

    for inner in range(per):
        send_first(b_hbm.at[inner, :, :, first_cols], inner)
    for inner in range(per):
        push(b_hbm.at[inner, :, :, second_cols], raw_pair.at[inner], raw_send.at[inner], raw_recv.at[inner], pair)

    mid = a_cap // 2
    y_up, y_down = at_y(1), at_y(-1)
    left, right, across = at_y(-1)[1], at_y(1)[1], at_y(2)[1]

    def own_a(first, slot, device):
        push(a_hbm.at[pl.ds(first, mid)], a_part(0, col, first), a_send.at[slot], a_recv.at[slot], device)

    own_a(0, 0, y_up)
    own_a(mid, 3, y_down)
    own_a(mid, 1, y_up)
    own_a(0, 4, y_down)
    for number in range(2):
        first, slot = number * mid, 12 + number
        push(a_hbm.at[pl.ds(first, mid)], a_part(1, col, first), a_send.at[slot], a_recv.at[slot], pair)
    local = [
        pltpu.make_async_copy(a_hbm, a_own.at[pl.ds(col * a_cap, a_cap)], local_sem.at[0]),
    ]
    for inner in range(per):
        local.append(
            pltpu.make_async_copy(b_hbm.at[inner, :, :, first_cols], b_unit(z, core, inner), local_sem.at[1 + inner])
        )
    local_raw = [
        pltpu.make_async_copy(b_hbm.at[inner, :, :, second_cols], raw_own.at[inner], local_sem.at[3 + inner])
        for inner in range(per)
    ]
    for made in local + local_raw:
        made.start()
    meta_x[dep] = meta[...]
    meta_y[0, col] = meta[...]
    meta_z[0, row] = meta[...]

    def forward_meta(step):
        for direction, limit in ((0, hops_up), (1, hops_down)):
            if step >= limit:
                continue
            origin_z = lax.rem(z - step - 1 + n_z, n_z) if direction == 0 else lax.rem(z + step + 1, n_z)
            here = meta_z.at[0, origin_z * 2 + core]
            index = ring_meta + 2 * step + direction
            pulled(here, meta_send.at[index], meta_recv.at[index])
            if step + 1 < limit:
                push(here, here, meta_send.at[index + 2], meta_recv.at[index + 2], up if direction == 0 else down)
            index = core_meta + 2 * step + direction
            push(here, here, meta_send.at[index], meta_recv.at[index], sibling)
            meta_waits.append((meta_z.at[0, origin_z * 2 + 1 - core], index))

    def pair_tables():
        for here, index in meta_waits:
            pulled(here, meta_send.at[index], meta_recv.at[index])
        push(meta_y.at[0], meta_y.at[1], meta_send.at[pair_meta], meta_recv.at[pair_meta], pair)
        push(meta_z.at[0], meta_z.at[1], meta_send.at[pair_meta + 1], meta_recv.at[pair_meta + 1], pair)

    core_waits = [[(b_unit(z, 1 - core, kind * per + inner), kind * per + inner) for inner in range(per)] for kind in range(2)]

    def pack(inner):
        pulled(raw_pair.at[inner], raw_send.at[inner], raw_recv.at[inner])
        base = (row * per + inner) * kb
        for t in range(kb):
            mine, other = raw_own[inner, t].astype(F32), raw_pair[inner, t].astype(F32)
            mine = jnp.where(side == 0, mine, pltpu.roll(mine, quarter, 1))
            other = jnp.where(side == 0, pltpu.roll(other, quarter, 1), other)
            b_second[base + t] = jnp.where(low_lanes, mine, other).astype(b_second.dtype)

    def forward_b(step, unit):
        for direction in range(2):
            limit = hops(direction, unit)
            if step >= limit:
                continue
            origin_z = lax.rem(z - step - 1 + n_z, n_z) if direction == 0 else lax.rem(z + step + 1, n_z)
            here = b_unit(origin_z, core, unit)
            index = ring_slot(direction, step, unit)
            pulled(here, ring_send.at[index], ring_recv.at[index])
            if step + 1 < limit:
                index = ring_slot(direction, step + 1, unit)
                push(here, here, ring_send.at[index], ring_recv.at[index], up if direction == 0 else down)
            index = n_u + ring_slot(direction, step, unit)
            push(here, here, core_send.at[index], core_recv.at[index], sibling)
            core_waits[units[unit][0]].append((b_unit(origin_z, 1 - core, unit), index))

    def arrived(kind, origin, first, slot):
        here = a_part(kind, origin, first)
        pulled(here, a_send.at[slot], a_recv.at[slot])
        return here

    def hand_on(here, slot, device):
        push(here, here, a_send.at[slot], a_recv.at[slot], device)

    def finish(kind):
        for here, index in core_waits[kind]:
            pulled(here, core_send.at[index], core_recv.at[index])

    def plan(kind, tab_int, tab_scale, ids, scales, sem):
        schedule(dims, kind, meta_x, meta_y, meta_z, tab_int, tab_scale)
        made = [
            pltpu.make_async_copy(tab_int, ids, local_sem.at[sem]),
            pltpu.make_async_copy(tab_scale, scales, local_sem.at[sem + 1]),
        ]
        for one in made:
            one.start()
        return made

    def bounded(index, size):
        return jnp.clip(index, 0, size - 1)

    def multiply(a_refs, b_refs, ids, scales, prod):
        n_p = kb * n_c
        acc[...] = jnp.zeros_like(acc)
        prod[n_p] = jnp.zeros(prod.shape[1:], prod.dtype)

        @pl.loop(0, n_p, unroll=16)
        def _(j):
            left_block = a_refs[bounded(ids[0, j], n_c)]
            right_block = b_refs[bounded(ids[1, j], n_g * kb)]
            product = jnp.dot(left_block, right_block, preferred_element_type=F32)
            total = acc[...] * scales[1, j] + product * scales[0, j]
            acc[...] = total
            prod[j] = total.astype(prod.dtype)

    piece = 2
    half_c = c_cap // 2
    steps = half_c // piece
    x_up, x_down = at_x(1), at_x(-1)
    d_right, d_left = x_up[2], x_down[2]
    dtype = result.dtype

    def own1(dest, index):
        return prod1[bounded(ids1[2, dest * c_cap + index], prod1.shape[0])]

    def part(refs, stage, k):
        return refs.at[pl.ds(stage * half_c + k * piece, piece)]

    def send_right(stage, k):
        index = stage * steps + k
        return copy(part(to_right, stage, k), part(from_left, stage, k), r_send.at[index], r_recv.at[index], x_up)

    def send_left(stage, k):
        index = stage * steps + k
        return copy(part(to_left, stage, k), part(from_right, stage, k), l_send.at[index], l_recv.at[index], x_down)

    def wait_left(stage, k):
        here, index = part(from_left, stage, k), stage * steps + k
        copy(here, here, r_send.at[index], r_recv.at[index], x_up).wait_recv()

    def wait_right(stage, k):
        here, index = part(from_right, stage, k), stage * steps + k
        copy(here, here, l_send.at[index], l_recv.at[index], x_down).wait_recv()

    def first_sends():
        @pl.loop(0, steps)
        def _(k):
            for i in range(piece):
                to_right[k * piece + i] = own1(d_far, k * piece + i)
            send_right(0, k).start()
            for i in range(piece):
                to_left[k * piece + i] = own1(d_far, half_c + k * piece + i)
            send_left(0, k).start()

        @pl.loop(0, steps)
        def _(k):
            for i in range(piece):
                to_right[half_c + k * piece + i] = own1(d_right, half_c + k * piece + i)
            send_right(1, k).start()
            for i in range(piece):
                to_left[half_c + k * piece + i] = own1(d_left, k * piece + i)
            send_left(1, k).start()

    def pass_sums(first, last):
        @pl.loop(first, last)
        def _(k):
            wait_left(0, k)
            for i in range(piece):
                m = k * piece + i
                total = own1(d_right, m).astype(F32) + from_left[m].astype(F32)
                to_right[2 * half_c + m] = total.astype(dtype)
            send_right(2, k).start()
            wait_right(0, k)
            for i in range(piece):
                m = k * piece + i
                total = own1(d_left, half_c + m).astype(F32) + from_right[m].astype(F32)
                to_left[2 * half_c + m] = total.astype(dtype)
            send_left(2, k).start()

    def first_results():
        @pl.loop(0, steps)
        def _(k):
            wait_right(1, k)
            wait_left(2, k)
            for i in range(piece):
                m = k * piece + i
                total = own1(dep, m).astype(F32) + from_left[2 * half_c + m].astype(F32)
                result[m, :, 0:half] = (total + from_right[half_c + m].astype(F32)).astype(dtype)
            wait_left(1, k)
            wait_right(2, k)
            for i in range(piece):
                m = k * piece + i
                total = own1(dep, half_c + m).astype(F32) + from_right[2 * half_c + m].astype(F32)
                result[half_c + m, :, 0:half] = (total + from_left[half_c + m].astype(F32)).astype(dtype)

    def packed(dest, u):
        def take(prod, ids, index):
            return prod[bounded(ids[2, dest * c_cap + index], prod.shape[0])].astype(F32)

        mine = take(prod2, ids1, u), take(prod2, ids1, half_c + u)
        other = take(prod3, ids2, u), take(prod3, ids2, half_c + u)
        straight, crossed = jnp.where(low_lanes, mine[0], other[1]), jnp.where(low_lanes, mine[1], other[0])
        return straight + pltpu.roll(crossed, quarter, 1)

    def send_mirror(stage, k):
        index = stage * steps + k
        return copy(part(to_mirror, stage, k), part(from_mirror, stage, k), m_send.at[index], m_recv.at[index], mirror)

    def send_pair(k):
        return copy(part(to_pair, 0, k), part(from_pair, 0, k), p_send.at[k], p_recv.at[k], pair)

    def write(number, k):
        here = pl.ds(number * half_c + k * piece, piece)
        return pltpu.make_async_copy(result.at[here], out_hbm.at[here], out_sem.at[number * steps + k])

    def second_sends():
        for stage, dest in ((0, d_far), (1, d_mirror)):

            @pl.loop(0, steps)
            def _(k):
                for i in range(piece):
                    u = k * piece + i
                    to_mirror[stage * half_c + u] = packed(dest, u).astype(dtype)
                send_mirror(stage, k).start()

    def second_results():
        @pl.loop(0, steps)
        def _(k):
            send_mirror(0, k).wait_recv()
            for i in range(piece):
                u = k * piece + i
                to_pair[u] = (packed(d_pair, u) + from_mirror[u].astype(F32)).astype(dtype)
            send_pair(k).start()

        @pl.loop(0, steps)
        def _(k):
            send_pair(k).wait_recv()
            send_mirror(1, k).wait_recv()
            for i in range(piece):
                u = k * piece + i
                mine = packed(dep, u) + from_mirror[half_c + u].astype(F32)
                other = from_pair[u].astype(F32)
                low = jnp.where(side == 0, mine, other)
                high = jnp.where(side == 0, other, mine)
                result[u, :, half : 2 * half] = jnp.where(low_lanes, low, pltpu.roll(high, quarter, 1)).astype(dtype)
                result[half_c + u, :, half : 2 * half] = jnp.where(
                    low_lanes, pltpu.roll(low, quarter, 1), high
                ).astype(dtype)
            write(0, k).start()
            write(1, k).start()

    forward_meta(0)
    forward_b(0, 0)
    for made in local_raw:
        made.wait()
    forward_b(0, 1)
    forward_meta(1)
    for inner in range(per):
        pack(inner)
    hand_on(arrived(0, left, 0, 0), 2, y_up)
    hand_on(arrived(0, right, mid, 3), 5, y_down)
    forward_b(1, 0)
    forward_meta(2)
    forward_b(1, 1)
    forward_meta(3)
    forward_b(2, 0)
    own_packed = [b_unit(z, core, per + inner) for inner in range(per)]
    send_first(own_packed[0], per)
    pair_tables()
    table1 = plan(0, tab_int1, tab_scale1, ids1, scales1, 5)
    forward_b(2, 1)
    send_first(own_packed[1], per + 1)
    arrived(0, left, mid, 1)
    arrived(0, right, 0, 4)
    low_a, high_a = arrived(1, col, 0, 12), arrived(1, col, mid, 13)
    hand_on(low_a, 6, y_up)
    hand_on(high_a, 9, y_down)
    hand_on(high_a, 7, y_up)
    hand_on(low_a, 10, y_down)
    forward_b(3, 0)
    forward_b(3, 1)
    arrived(0, across, 0, 2)
    arrived(0, across, mid, 5)
    for made in table1 + local:
        made.wait()
    finish(0)
    forward_b(0, 2)
    multiply(a_own, b_first, ids1, scales1, prod1)
    first_sends()
    forward_b(0, 3)
    hand_on(arrived(1, left, 0, 6), 8, y_up)
    hand_on(arrived(1, right, mid, 9), 11, y_down)
    forward_b(1, 2)
    pulled(meta_y.at[1], meta_send.at[pair_meta], meta_recv.at[pair_meta])
    pulled(meta_z.at[1], meta_send.at[pair_meta + 1], meta_recv.at[pair_meta + 1])
    table2 = plan(1, tab_int2, tab_scale2, ids2, scales2, 7)
    forward_b(1, 3)
    pass_sums(0, 2)
    forward_b(2, 2)
    pass_sums(2, 4)
    forward_b(2, 3)
    pass_sums(4, steps)
    forward_b(3, 2)
    forward_b(3, 3)
    finish(1)
    multiply(a_own, b_second, ids1, scales1, prod2)
    arrived(1, left, mid, 7)
    arrived(1, right, 0, 10)
    arrived(1, across, 0, 8)
    arrived(1, across, mid, 11)
    for made in table2:
        made.wait()
    multiply(a_pair, b_second, ids2, scales2, prod3)
    second_sends()
    first_results()
    second_results()

    @pl.loop(0, steps)
    def _(k):
        write(0, k).wait()
        write(1, k).wait()
        send_pair(k).wait_send()
        for stage in range(2):
            send_mirror(stage, k).wait_send()
        for stage in range(3):
            send_right(stage, k).wait_send()
            send_left(stage, k).wait_send()

    for made in sends:
        made.wait_send()


def shards(a_blocks, a_scale, a_rows, a_cols, b_blocks, b_scale, b_cols, c_rows, c_cols):
    edge = a_blocks.shape[1]
    half = edge // 2
    a_cap, c_cap = a_blocks.shape[0], c_rows.shape[0]
    per, kb = b_blocks.shape[0], b_blocks.shape[3]
    n_r, n_y, n_x = lax.axis_size("row"), lax.axis_size("col"), lax.axis_size("depth")
    dims = (n_x, n_y, n_r, a_cap, per, kb, c_cap)
    n_c = n_y * a_cap
    half_c = c_cap // 2

    width = -(-kb * n_c // LANES) * LANES

    dtype = a_blocks.dtype
    block, part = (edge, edge), (edge, half)
    dma = pltpu.SemaphoreType.DMA
    hops = n_r // 4
    n_meta = (n_y - 1) + (n_x - 1) + 1 + 4 * hops + 2
    n_ring = 2 * hops * 2 * per
    any_space = pl.BlockSpec(memory_space=pl.ANY)
    vmem = pl.BlockSpec(memory_space=pltpu.VMEM)
    return pl.pallas_call(
        functools.partial(kernel, dims),
        out_shape=jax.ShapeDtypeStruct((c_cap,) + block, dtype),
        in_specs=[any_space, any_space] + [vmem] * 7,
        out_specs=any_space,
        scratch_shapes=[
            pltpu.VMEM((n_c,) + block, dtype),
            pltpu.VMEM((n_c,) + block, dtype),
            pltpu.VMEM((n_r * per * kb,) + part, dtype),
            pltpu.VMEM((n_r * per * kb,) + part, dtype),
            pltpu.VMEM((per, kb) + part, dtype),
            pltpu.VMEM((per, kb) + part, dtype),
            pltpu.VMEM((8, LANES), F32),
            pltpu.VMEM((n_x, 8, LANES), F32),
            pltpu.VMEM((2, n_y, 8, LANES), F32),
            pltpu.VMEM((2, n_r, 8, LANES), F32),
        ]
        + [
            space((8, width), kind)
            for _ in range(2)
            for space in (pltpu.VMEM, pltpu.SMEM)
            for kind in (jnp.int32, F32)
        ]
        + [
            pltpu.VMEM(part, F32),
        ]
        + [pltpu.VMEM((kb * n_c + 1,) + part, dtype)] * 3
        + [pltpu.VMEM((3 * half_c,) + part, dtype)] * 4
        + [pltpu.VMEM((2 * half_c,) + part, dtype)] * 2
        + [pltpu.VMEM((half_c,) + part, dtype)] * 2
        + [
            pltpu.VMEM((c_cap,) + block, dtype),
            dma((9,)),
            dma((n_meta,)),
            dma((n_meta,)),
            dma((n_ring,)),
            dma((n_ring,)),
            dma((2 * per + n_ring,)),
            dma((2 * per + n_ring,)),
            dma((per,)),
            dma((per,)),
            dma((14,)),
            dma((14,)),
        ]
        + [dma((3 * half_c,))] * 4
        + [dma((2 * half_c,))] * 2
        + [dma((half_c,))] * 2
        + [dma((c_cap,))],
        compiler_params=pltpu.CompilerParams(
            collective_id=0, has_side_effects=True, vmem_limit_bytes=62 * 1024 * 1024
        ),
    )(
        a_blocks,
        b_blocks.reshape(per, kb, edge, edge),
        a_scale.reshape(1, a_cap),
        a_rows.reshape(1, a_cap),
        a_cols.reshape(1, a_cap),
        b_scale.reshape(per, kb),
        b_cols.reshape(per, kb),
        c_rows.reshape(1, c_cap),
        c_cols.reshape(1, c_cap),
    )


def solution(mesh):
    return jax.shard_map(
        shards,
        mesh=mesh,
        in_specs=(
            P(("row", "col", "depth"), None, None),
            P(("row", "col", "depth")),
            P(("row", "col", "depth")),
            P(("row", "col", "depth")),
            P("row", "col", "depth", None, None, None),
            P("row", "col", "depth", None),
            P("row", "col", "depth", None),
            P(("row", "col", "depth")),
            P(("row", "col", "depth")),
        ),
        out_specs=P(("row", "col", "depth"), None, None),
        check_vma=False,
    )
```

time: 150 us -> 130 us (0.87)
  Pallas kernels: 146 us -> 125 us
    pallas_call x1, Pallas kernels: 146 us -> 125 us  [shards(): pl.pallas_call(functools.partial(kernel, dims), out_shape=jax.ShapeDtypeS...]
where the time goes in v3:
time: 130 us; the launch traced here: 128 us
  Pallas kernels  125 us (96%)
  local copies, waits for them, and re-layouts  3.47 us (3%)
    pallas_call x1, Pallas kernels, shards(): pl.pallas_call(functools.partial(kernel, dims), out_shape=jax.ShapeDtypeS...  125 us
    unnamed x1, local copies, waits for them, and re-layouts  3.47 us

profile of v3, /device:TPU:1, one launch (start us, length us, event | category | flops | bytes accessed | tf_op | source)
XLA Modules:
  0.0 128.3 jit_solution(3098589455585947287)
XLA Ops:
  0.0 124.9 %shard_map.91 = bf16[20,256,256]{2,1,0:T(8,128)(2,1)} custom-call(bf16[8,256,256]{2,1,0:T(8,128)(2,1)} %a_hbm.1, bf16[2,3,256,256]{3,2,1,0:T(8,128)(2,1)} %bitcast.8, f32[1,8]{1,0:T(1,128)} %bitcast.11, s32[1,8]{1,0:T(1,128)} %bitcast.12, s32[1,8]{1,0:T(1,128)} %bitcast.13, f32[2,3]{1,0:T(2,128)} %bitcast.9, s32[2,3]{1,0:T(2,128)} %bitcast.10, ...), custom_call_target="tpu_custom_call" | custom-call | tf_op jit(solution)/shard_map/pallas_call | solution.py:559
  124.9 3.5 %copy.11 = bf16[20,256,256]{2,1,0:T(8,128)(2,1)} copy(bf16[20,256,256]{2,1,0:T(8,128)(2,1)} %shard_map.91) | data formatting | bytes 5242880

commit v4 on v3

v4 whole, which is shorter than its diff:
```python
import functools

import jax
import jax.numpy as jnp
from jax import lax
from jax.experimental import pallas as pl
from jax.experimental.pallas import tpu as pltpu
from jax.sharding import PartitionSpec as P

MESH = pl.DeviceIdType.MESH
LANES = 128
ROW_KEY = 1024.0
F32 = jnp.float32


def iota(shape, dim):
    return lax.broadcasted_iota(jnp.int32, shape, dim)


def schedule(dims, kind, meta_x, meta_y, meta_z, tab_int, tab_scale):
    n_x, n_y, n_r, a_cap, per, kb, c_cap = dims
    n_a = n_y * a_cap
    n_g = n_r * per
    n_slots = n_x * c_cap
    eye = iota((a_cap, LANES), 0) == iota((a_cap, LANES), 1)
    lane = iota((n_a, LANES), 1)

    def column(which):
        parts = [
            jnp.sum(jnp.where(eye, meta_y[kind, c, which : which + 1, :], 0.0), axis=1, keepdims=True)
            for c in range(n_y)
        ]
        return jnp.concatenate(parts, axis=0)

    a_scale, a_rows, a_cols = column(0), column(1), column(2)
    group = a_cols.astype(jnp.int32) // n_x
    b_scale = jnp.zeros((n_a, LANES), F32)
    b_cols = jnp.zeros((n_a, LANES), F32)
    for g in range(n_g):
        here = group == g
        d, i = g // per, g % per
        b_scale = jnp.where(here, meta_z[kind, d, 3 + i : 4 + i, :], b_scale)
        b_cols = jnp.where(here, meta_z[kind, d, 5 + i : 6 + i, :], b_cols)
    device, inner = group // per, group % per
    slots, weights, b_ids, first_ids = [], [], [], []
    for t in range(kb):
        col = jnp.sum(jnp.where(lane == t, b_cols, 0.0), axis=1, keepdims=True)
        scale = jnp.sum(jnp.where(lane == t, b_scale, 0.0), axis=1, keepdims=True)
        key = a_rows * ROW_KEY + col
        found = jnp.zeros((n_a, LANES), F32)
        for e in range(n_x):
            hit = (key == meta_x[e, 7:8, :]) & (lane < c_cap)
            found = jnp.where(hit, (lane + (e * c_cap + 1)).astype(F32), found)
        slot = jnp.max(found, axis=1, keepdims=True)
        slots.append(jnp.where(slot > 0, slot - 1, float(n_slots)))
        weights.append(a_scale * scale)
        b_ids.append((group * kb + t).astype(F32))
        first_ids.append((device * kb + t).astype(F32))
    slot, weight = jnp.concatenate(slots, axis=0), jnp.concatenate(weights, axis=0)
    a_id = jnp.concatenate([iota((n_a, 1), 0).astype(F32)] * kb, axis=0)
    b_id, first_id = jnp.concatenate(b_ids, axis=0), jnp.concatenate(first_ids, axis=0)
    low = jnp.where(jnp.concatenate([inner] * kb, axis=0) == 0, weight, 0.0)
    n_p = kb * n_a
    width = tab_int.shape[1]
    place, lane = iota((n_p, width), 0), iota((n_p, width), 1)
    row_slot = jnp.sum(jnp.where(place == lane, slot, 0.0), axis=0, keepdims=True)
    row_slot = jnp.where(lane[:1] < n_p, row_slot, 1e6)
    earlier = (row_slot == slot) & (lane < place)
    before = (row_slot < slot) | earlier
    rank = jnp.sum(jnp.where(before, 1.0, 0.0), axis=1, keepdims=True)
    keep = jnp.where(jnp.sum(jnp.where(earlier, 1.0, 0.0), axis=1, keepdims=True) > 0, 1.0, 0.0)
    lane_f = lane.astype(F32)
    mine = rank == lane_f

    def ordered(values):
        return jnp.sum(jnp.where(mine, values, 0.0), axis=0, keepdims=True)

    last = jnp.sum(jnp.where(slot <= lane_f, 1.0, 0.0), axis=0, keepdims=True) - 1.0
    some = jnp.sum(jnp.where(slot == lane_f, 1.0, 0.0), axis=0, keepdims=True)
    last = jnp.where(some > 0, last, float(n_p))
    zero = jnp.zeros((1, width), F32)
    table = jnp.concatenate(
        [ordered(a_id), ordered(b_id), last, ordered(first_id), zero, zero, zero, zero], axis=0
    ).astype(jnp.int32)
    which = iota(table.shape, 0)
    top = jnp.where(which == 0, n_a - 1, jnp.where(which == 1, n_g * kb - 1, n_p))
    top = jnp.where(which == 3, n_r * kb - 1, top)
    tab_int[...] = jnp.clip(table, 0, top)
    tab_scale[...] = jnp.concatenate(
        [ordered(weight), ordered(keep), ordered(low), ordered(weight - low), zero, zero, zero, zero], axis=0
    )


def kernel(
    dims, a_hbm, b_hbm, a_scale, a_rows, a_cols, b_scale, b_cols, c_rows, c_cols, out_hbm,
    a_own0, a_own1, a_pair0, a_pair1, b_one, b_two, b_second, raw_own, raw_pair, meta, meta_x, meta_y, meta_z,
    tab_int1, tab_scale1, ids1, scales1, tab_int2, tab_scale2, ids2, scales2,
    acc, prod0, prod1, prod2, prod3, prod4, prod5, prod6, prod7,
    to_right, to_left, from_left, from_right, to_mirror, from_mirror, to_pair, from_pair, result,
    local_sem, meta_send, meta_recv, ring_send, ring_recv, core_send, core_recv, raw_send, raw_recv, a_send, a_recv,
    r_send, r_recv, l_send, l_recv, m_send, m_recv, p_send, p_recv, out_sem,
):
    n_x, n_y, n_r, a_cap, per, kb, c_cap = dims
    n_z = n_r // 2
    n_g = n_r * per
    n_c = n_y * a_cap
    half = b_second.shape[2]
    quarter = half // 2
    a_own, a_pair = (a_own0, a_own1), (a_pair0, a_pair1)
    first_prod = ((prod0, prod1), (prod2, prod3))
    own_prod, pair_prod = (prod4, prod5), (prod6, prod7)
    row, col, dep = lax.axis_index("row"), lax.axis_index("col"), lax.axis_index("depth")
    z, core = row // 2, row % 2

    def at_z(step):
        return (lax.rem(z + step + n_z, n_z) * 2 + core, col, dep)

    def at_y(step):
        return (row, lax.rem(col + step + n_y, n_y), dep)

    def at_x(step):
        return (row, col, lax.rem(dep + step + n_x, n_x))

    sibling = (z * 2 + 1 - core, col, dep)
    d_pair, d_mirror, d_far = dep + 1 - 2 * (dep % 2), n_x - 1 - dep, lax.rem(dep + 2, n_x)
    pair, mirror = (row, col, d_pair), (row, col, d_mirror)
    side = ((dep + 1) // 2) % 2
    second_cols = pl.ds(half, half)
    low_lanes = iota((1, half), 1) < quarter

    meta[...] = jnp.zeros_like(meta)
    meta[0:1, 0:a_cap] = a_scale[...]
    meta[1:2, 0:a_cap] = a_rows[...].astype(F32)
    meta[2:3, 0:a_cap] = a_cols[...].astype(F32)
    meta[3 : 3 + per, 0:kb] = b_scale[...]
    meta[5 : 5 + per, 0:kb] = b_cols[...].astype(F32)
    meta[7:8, 0:c_cap] = c_rows[...].astype(F32) * ROW_KEY + c_cols[...].astype(F32)

    barrier = pltpu.get_barrier_semaphore()
    partners = [sibling, at_z(1), at_z(-1)] + [at_y(j) for j in range(1, n_y)] + [at_x(j) for j in range(1, n_x)]
    for partner in partners:
        pl.semaphore_signal(barrier, inc=1, device_id=partner, device_id_type=MESH)
    local_raw = pltpu.make_async_copy(b_hbm, raw_own, local_sem.at[0])
    local_raw.start()
    local_raw.wait()
    for t in range(kb):
        one, two = raw_own[0, t, :, 0:half].astype(F32), raw_own[1, t, :, 0:half].astype(F32)
        b_one[row * kb + t] = jnp.where(low_lanes, one, pltpu.roll(two, quarter, 1)).astype(b_one.dtype)
        b_two[row * kb + t] = jnp.where(low_lanes, pltpu.roll(one, quarter, 1), two).astype(b_two.dtype)
    pl.semaphore_wait(barrier, len(partners))

    sends = []

    def copy(src, dst, send, recv, device):
        return pltpu.make_async_remote_copy(
            src_ref=src, dst_ref=dst, send_sem=send, recv_sem=recv, device_id=device, device_id_type=MESH
        )

    def push(src, dst, send, recv, device):
        made = copy(src, dst, send, recv, device)
        made.start()
        sends.append(made)

    def pulled(dst, send, recv):
        copy(dst, dst, send, recv, sibling).wait_recv()

    count = 0
    meta_waits = []
    for j in range(1, n_y):
        push(meta, meta_y.at[0, col], meta_send.at[count], meta_recv.at[count], at_y(j))
        meta_waits.append((meta_y.at[0, lax.rem(col - j + n_y, n_y)], count))
        count += 1
    for j in range(1, n_x):
        push(meta, meta_x.at[dep], meta_send.at[count], meta_recv.at[count], at_x(j))
        meta_waits.append((meta_x.at[lax.rem(dep - j + n_x, n_x)], count))
        count += 1
    push(meta, meta_z.at[0, row], meta_send.at[count], meta_recv.at[count], sibling)
    meta_waits.append((meta_z.at[0, z * 2 + 1 - core], count))
    count += 1
    hops_up, hops_down = n_z // 2, (n_z - 1) // 2
    ring_meta = count
    push(meta, meta_z.at[0, row], meta_send.at[count], meta_recv.at[count], at_z(1))
    push(meta, meta_z.at[0, row], meta_send.at[count + 1], meta_recv.at[count + 1], at_z(-1))
    count += 2 * hops_up
    core_meta = count
    count += 2 * hops_up
    pair_meta = count

    up, down = at_z(1), at_z(-1)
    units = [(b_one, kb, t, 1, t // 2) for t in range(kb)]
    units += [(b_two, kb, t, 1, 1 - t // 2) for t in range(kb)]
    units += [(b_second, per * kb, inner * kb, kb, inner) for inner in range(per)]
    n_u = len(units)
    unit_one, unit_two = list(range(kb)), list(range(kb, 2 * kb))
    unit_second = list(range(2 * kb, 2 * kb + per))

    def b_unit(origin_z, origin_core, unit):
        refs, each, first, size, _ = units[unit]
        return refs.at[pl.ds((origin_z * 2 + origin_core) * each + first, size)]

    def a_part(refs, origin, first):
        return refs.at[pl.ds(origin * a_cap + first, a_cap // 2)]

    def ring_slot(direction, step, unit):
        return (direction * hops_up + step) * n_u + unit

    def hops(direction, unit):
        return hops_up if units[unit][4] == direction else hops_down

    def send_first(src, unit):
        for direction, device in ((0, up), (1, down)):
            index = ring_slot(direction, 0, unit)
            push(src, b_unit(z, core, unit), ring_send.at[index], ring_recv.at[index], device)
        push(src, b_unit(z, core, unit), core_send.at[unit], core_recv.at[unit], sibling)

    for unit in unit_one:
        send_first(b_unit(z, core, unit), unit)
    for inner in range(per):
        push(raw_own.at[inner, :, :, second_cols], raw_pair.at[inner], raw_send.at[inner], raw_recv.at[inner], pair)

    mid = a_cap // 2
    y_up, y_down = at_y(1), at_y(-1)
    left, right, across = at_y(-1)[1], at_y(1)[1], at_y(2)[1]

    def a_rows_of(rr, first):
        return a_hbm.at[pl.ds(first, mid), pl.ds(rr * half, half)]

    def send_own_a(rr):
        for first, slot, device in ((0, 0, y_up), (mid, 3, y_down), (mid, 1, y_up), (0, 4, y_down)):
            index = rr * 14 + slot
            push(a_rows_of(rr, first), a_part(a_own[rr], col, first), a_send.at[index], a_recv.at[index], device)

    def send_raw_a(rr):
        for number in range(2):
            first, index = number * mid, rr * 14 + 12 + number
            push(a_rows_of(rr, first), a_part(a_pair[rr], col, first), a_send.at[index], a_recv.at[index], pair)

    send_own_a(0)
    send_raw_a(0)
    local = [
        pltpu.make_async_copy(
            a_hbm.at[:, pl.ds(rr * half, half)], a_own[rr].at[pl.ds(col * a_cap, a_cap)], local_sem.at[1 + rr]
        )
        for rr in range(2)
    ]
    for made in local:
        made.start()
    meta_x[dep] = meta[...]
    meta_y[0, col] = meta[...]
    meta_z[0, row] = meta[...]

    def forward_meta(step):
        for direction, limit in ((0, hops_up), (1, hops_down)):
            if step >= limit:
                continue
            origin_z = lax.rem(z - step - 1 + n_z, n_z) if direction == 0 else lax.rem(z + step + 1, n_z)
            here = meta_z.at[0, origin_z * 2 + core]
            index = ring_meta + 2 * step + direction
            pulled(here, meta_send.at[index], meta_recv.at[index])
            if step + 1 < limit:
                push(here, here, meta_send.at[index + 2], meta_recv.at[index + 2], up if direction == 0 else down)
            index = core_meta + 2 * step + direction
            push(here, here, meta_send.at[index], meta_recv.at[index], sibling)
            meta_waits.append((meta_z.at[0, origin_z * 2 + 1 - core], index))

    def pair_tables():
        for here, index in meta_waits:
            pulled(here, meta_send.at[index], meta_recv.at[index])
        push(meta_y.at[0], meta_y.at[1], meta_send.at[pair_meta], meta_recv.at[pair_meta], pair)
        push(meta_z.at[0], meta_z.at[1], meta_send.at[pair_meta + 1], meta_recv.at[pair_meta + 1], pair)

    core_waits = [[(b_unit(z, 1 - core, unit), unit)] for unit in range(n_u)]

    def pack(inner):
        pulled(raw_pair.at[inner], raw_send.at[inner], raw_recv.at[inner])
        base = (row * per + inner) * kb
        for t in range(kb):
            mine, other = raw_own[inner, t, :, half : 2 * half].astype(F32), raw_pair[inner, t].astype(F32)
            mine = jnp.where(side == 0, mine, pltpu.roll(mine, quarter, 1))
            other = jnp.where(side == 0, pltpu.roll(other, quarter, 1), other)
            b_second[base + t] = jnp.where(low_lanes, mine, other).astype(b_second.dtype)

    def forward_b(step, unit):
        for direction in range(2):
            limit = hops(direction, unit)
            if step >= limit:
                continue
            origin_z = lax.rem(z - step - 1 + n_z, n_z) if direction == 0 else lax.rem(z + step + 1, n_z)
            here = b_unit(origin_z, core, unit)
            index = ring_slot(direction, step, unit)
            pulled(here, ring_send.at[index], ring_recv.at[index])
            if step + 1 < limit:
                index = ring_slot(direction, step + 1, unit)
                push(here, here, ring_send.at[index], ring_recv.at[index], up if direction == 0 else down)
            index = n_u + ring_slot(direction, step, unit)
            push(here, here, core_send.at[index], core_recv.at[index], sibling)
            core_waits[unit].append((b_unit(origin_z, 1 - core, unit), index))

    def arrived(refs, rr, origin, first, slot):
        here, index = a_part(refs[rr], origin, first), rr * 14 + slot
        pulled(here, a_send.at[index], a_recv.at[index])
        return here

    def hand_on(here, rr, slot, device):
        index = rr * 14 + slot
        push(here, here, a_send.at[index], a_recv.at[index], device)

    def across_a(refs, rr, base):
        hand_on(arrived(refs, rr, left, 0, base), rr, base + 2, y_up)
        hand_on(arrived(refs, rr, right, mid, base + 3), rr, base + 5, y_down)

    def rest_a(refs, rr, base):
        arrived(refs, rr, left, mid, base + 1)
        arrived(refs, rr, right, 0, base + 4)
        arrived(refs, rr, across, 0, base + 2)
        arrived(refs, rr, across, mid, base + 5)

    def spread_pair_a(rr):
        low_a, high_a = arrived(a_pair, rr, col, 0, 12), arrived(a_pair, rr, col, mid, 13)
        hand_on(low_a, rr, 6, y_up)
        hand_on(high_a, rr, 9, y_down)
        hand_on(high_a, rr, 7, y_up)
        hand_on(low_a, rr, 10, y_down)

    def finish(unit):
        for here, index in core_waits[unit]:
            pulled(here, core_send.at[index], core_recv.at[index])

    def plan(kind, tab_int, tab_scale, ids, scales, sem):
        schedule(dims, kind, meta_x, meta_y, meta_z, tab_int, tab_scale)
        made = [
            pltpu.make_async_copy(tab_int, ids, local_sem.at[sem]),
            pltpu.make_async_copy(tab_scale, scales, local_sem.at[sem + 1]),
        ]
        for one in made:
            one.start()
        return made

    def bounded(index, size):
        return jnp.clip(index, 0, size - 1)

    def multiply(a_refs, b_refs, ids, scales, prod, split):
        n_p = kb * n_c
        acc[...] = jnp.zeros_like(acc)
        prod[n_p] = jnp.zeros(prod.shape[1:], prod.dtype)

        @pl.loop(0, n_p, unroll=16)
        def _(j):
            left_block = a_refs[bounded(ids[0, j], n_c)]
            right_block = b_refs[bounded(ids[3 if split else 1, j], b_refs.shape[0])]
            product = jnp.dot(left_block, right_block, preferred_element_type=F32)
            weight = jnp.where(low_lanes, scales[2, j], scales[3, j]) if split else scales[0, j]
            total = acc[...] * scales[1, j] + product * weight
            acc[...] = total
            prod[j] = total.astype(prod.dtype)

    def folded(mine, other, dest, u, v):
        def take(which, index):
            prod, ids = which
            return prod[bounded(ids[2, dest * c_cap + index], prod.shape[0])].astype(F32)

        straight = jnp.where(low_lanes, take(mine, u), take(other, v))
        crossed = jnp.where(low_lanes, take(mine, v), take(other, u))
        return straight + pltpu.roll(crossed, quarter, 1)

    half_c = c_cap // 2
    pairs = half_c // 2
    x_up, x_down = at_x(1), at_x(-1)
    d_right, d_left = x_up[2], x_down[2]
    dtype = result.dtype

    def first_block(tile, dest, base, i):
        both = (first_prod[tile // 2][tile % 2], ids1)
        return folded(both, both, dest, base + i, base + pairs + i)

    def part(refs, tile, stage):
        return refs.at[pl.ds((tile * 3 + stage) * pairs, pairs)]

    def send_right(tile, stage):
        index = tile * 3 + stage
        return copy(part(to_right, tile, stage), part(from_left, tile, stage), r_send.at[index], r_recv.at[index], x_up)

    def send_left(tile, stage):
        index = tile * 3 + stage
        return copy(part(to_left, tile, stage), part(from_right, tile, stage), l_send.at[index], l_recv.at[index], x_down)

    def wait_left(tile, stage):
        here, index = part(from_left, tile, stage), tile * 3 + stage
        copy(here, here, r_send.at[index], r_recv.at[index], x_up).wait_recv()

    def wait_right(tile, stage):
        here, index = part(from_right, tile, stage), tile * 3 + stage
        copy(here, here, l_send.at[index], l_recv.at[index], x_down).wait_recv()

    def first_sends(tile):
        at = tile * 3 * pairs

        @pl.loop(0, pairs)
        def _(i):
            to_right[at + i] = first_block(tile, d_far, 0, i).astype(dtype)

        send_right(tile, 0).start()

        @pl.loop(0, pairs)
        def _(i):
            to_left[at + i] = first_block(tile, d_far, half_c, i).astype(dtype)

        send_left(tile, 0).start()

        @pl.loop(0, pairs)
        def _(i):
            to_right[at + pairs + i] = first_block(tile, d_right, half_c, i).astype(dtype)

        send_right(tile, 1).start()

        @pl.loop(0, pairs)
        def _(i):
            to_left[at + pairs + i] = first_block(tile, d_left, 0, i).astype(dtype)

        send_left(tile, 1).start()

    def pass_sums(tile):
        at = tile * 3 * pairs
        wait_left(tile, 0)

        @pl.loop(0, pairs)
        def _(i):
            total = first_block(tile, d_right, 0, i) + from_left[at + i].astype(F32)
            to_right[at + 2 * pairs + i] = total.astype(dtype)

        send_right(tile, 2).start()
        wait_right(tile, 0)

        @pl.loop(0, pairs)
        def _(i):
            total = first_block(tile, d_left, half_c, i) + from_right[at + i].astype(F32)
            to_left[at + 2 * pairs + i] = total.astype(dtype)

        send_left(tile, 2).start()

    def first_results(rr):
        tiles = (rr, 2 + rr)
        rows = slice(rr * half, (rr + 1) * half)
        for tile in tiles:
            for stage in (1, 2):
                wait_right(tile, stage)
                wait_left(tile, stage)
        for base, left_stage, right_stage in ((0, 2, 1), (half_c, 1, 2)):

            @pl.loop(0, pairs)
            def _(i):
                one, two = [
                    first_block(tile, dep, base, i)
                    + from_left[(tile * 3 + left_stage) * pairs + i].astype(F32)
                    + from_right[(tile * 3 + right_stage) * pairs + i].astype(F32)
                    for tile in tiles
                ]
                result[base + i, rows, 0:half] = jnp.where(low_lanes, one, pltpu.roll(two, quarter, 1)).astype(dtype)
                result[base + pairs + i, rows, 0:half] = jnp.where(
                    low_lanes, pltpu.roll(one, quarter, 1), two
                ).astype(dtype)

    def packed(rr, dest, u):
        return folded((own_prod[rr], ids1), (pair_prod[rr], ids2), dest, u, half_c + u)

    def second_part(refs, rr, stage, k, stages):
        return refs.at[pl.ds((rr * stages + stage) * half_c + k * pairs, pairs)]

    def send_mirror(rr, stage, k):
        index = (rr * 2 + stage) * 2 + k
        return copy(
            second_part(to_mirror, rr, stage, k, 2), second_part(from_mirror, rr, stage, k, 2),
            m_send.at[index], m_recv.at[index], mirror,
        )

    def send_pair(rr, k):
        index = rr * 2 + k
        return copy(
            second_part(to_pair, rr, 0, k, 1), second_part(from_pair, rr, 0, k, 1),
            p_send.at[index], p_recv.at[index], pair,
        )

    def second_sends(rr, stage):
        dest = (d_far, d_mirror)[stage]
        for k in range(2):

            @pl.loop(0, pairs)
            def _(i):
                u = k * pairs + i
                to_mirror[(rr * 2 + stage) * half_c + u] = packed(rr, dest, u).astype(dtype)

            send_mirror(rr, stage, k).start()

    def second_sums(rr):
        for k in range(2):
            send_mirror(rr, 0, k).wait_recv()

            @pl.loop(0, pairs)
            def _(i):
                u = k * pairs + i
                total = packed(rr, d_pair, u) + from_mirror[rr * 2 * half_c + u].astype(F32)
                to_pair[rr * half_c + u] = total.astype(dtype)

            send_pair(rr, k).start()

    def write(rr, k):
        rows = pl.ds(rr * half, half)
        return [
            pltpu.make_async_copy(
                result.at[pl.ds(first + k * pairs, pairs), rows], out_hbm.at[pl.ds(first + k * pairs, pairs), rows],
                out_sem.at[(rr * 2 + k) * 2 + number],
            )
            for number, first in enumerate((0, half_c))
        ]

    def second_results(rr):
        rows = slice(rr * half, (rr + 1) * half)
        for k in range(2):
            send_pair(rr, k).wait_recv()
            send_mirror(rr, 1, k).wait_recv()

            @pl.loop(0, pairs)
            def _(i):
                u = k * pairs + i
                mine = packed(rr, dep, u) + from_mirror[(rr * 2 + 1) * half_c + u].astype(F32)
                other = from_pair[rr * half_c + u].astype(F32)
                low = jnp.where(side == 0, mine, other)
                high = jnp.where(side == 0, other, mine)
                result[u, rows, half : 2 * half] = jnp.where(low_lanes, low, pltpu.roll(high, quarter, 1)).astype(dtype)
                result[half_c + u, rows, half : 2 * half] = jnp.where(
                    low_lanes, pltpu.roll(low, quarter, 1), high
                ).astype(dtype)

            for made in write(rr, k):
                made.start()

    forward_b(0, unit_one[0])
    forward_b(0, unit_one[1])
    forward_b(0, unit_one[2])
    forward_meta(0)
    pack(0)
    across_a(a_own, 0, 0)
    send_first(b_unit(z, core, unit_two[0]), unit_two[0])
    send_first(b_unit(z, core, unit_two[2]), unit_two[2])
    forward_meta(1)
    send_first(b_unit(z, core, unit_two[1]), unit_two[1])
    forward_b(0, unit_two[0])
    forward_meta(2)
    forward_b(1, unit_one[1])
    forward_b(1, unit_one[2])
    pack(1)
    send_own_a(1)
    forward_b(0, unit_two[2])
    forward_meta(3)
    forward_b(1, unit_one[0])
    forward_b(0, unit_two[1])
    forward_b(2, unit_one[1])
    rest_a(a_own, 0, 0)
    send_raw_a(1)
    forward_b(1, unit_two[0])
    forward_b(2, unit_one[2])
    forward_b(2, unit_one[0])
    pair_tables()
    table1 = plan(0, tab_int1, tab_scale1, ids1, scales1, 3)
    forward_b(3, unit_one[1])
    send_first(b_unit(z, core, unit_second[0]), unit_second[0])
    forward_b(1, unit_two[2])
    forward_b(3, unit_one[2])
    forward_b(1, unit_two[1])
    across_a(a_own, 1, 0)
    finish(unit_one[1])
    forward_b(2, unit_two[0])
    forward_b(3, unit_one[0])
    for made in table1 + local:
        made.wait()
    finish(unit_one[2])
    send_first(b_unit(z, core, unit_second[1]), unit_second[1])
    spread_pair_a(0)
    finish(unit_one[0])
    multiply(a_own[0], b_one, ids1, scales1, prod0, True)
    first_sends(0)
    forward_b(2, unit_two[1])
    forward_b(2, unit_two[2])
    spread_pair_a(1)
    forward_b(0, unit_second[0])
    rest_a(a_own, 1, 0)
    multiply(a_own[1], b_one, ids1, scales1, prod1, True)
    first_sends(1)
    forward_b(3, unit_two[2])
    finish(unit_two[2])
    pass_sums(0)
    forward_b(3, unit_two[0])
    forward_b(0, unit_second[1])
    forward_b(3, unit_two[1])
    finish(unit_two[0])
    forward_b(1, unit_second[0])
    finish(unit_two[1])
    multiply(a_own[1], b_two, ids1, scales1, prod3, True)
    first_sends(3)
    across_a(a_pair, 0, 6)
    forward_b(1, unit_second[1])
    multiply(a_own[0], b_two, ids1, scales1, prod2, True)
    forward_b(2, unit_second[0])
    first_sends(2)
    pass_sums(1)
    forward_b(2, unit_second[1])
    pulled(meta_y.at[1], meta_send.at[pair_meta], meta_recv.at[pair_meta])
    pulled(meta_z.at[1], meta_send.at[pair_meta + 1], meta_recv.at[pair_meta + 1])
    table2 = plan(1, tab_int2, tab_scale2, ids2, scales2, 5)
    pass_sums(3)
    across_a(a_pair, 1, 6)
    forward_b(3, unit_second[0])
    forward_b(3, unit_second[1])
    finish(unit_second[0])
    for made in table2:
        made.wait()
    finish(unit_second[1])
    multiply(a_own[0], b_second, ids1, scales1, prod4, False)
    rest_a(a_pair, 0, 6)
    pass_sums(2)
    multiply(a_pair[0], b_second, ids2, scales2, prod6, False)
    rest_a(a_pair, 1, 6)
    second_sends(0, 0)
    first_results(1)
    second_sends(0, 1)
    multiply(a_pair[1], b_second, ids2, scales2, prod7, False)
    multiply(a_own[1], b_second, ids1, scales1, prod5, False)
    second_sums(0)
    second_sends(1, 0)
    second_sends(1, 1)
    first_results(0)
    second_sums(1)
    second_results(0)
    second_results(1)

    for rr in range(2):
        for k in range(2):
            for made in write(rr, k):
                made.wait()
            send_pair(rr, k).wait_send()
            for stage in range(2):
                send_mirror(rr, stage, k).wait_send()
    for tile in range(4):
        for stage in range(3):
            send_right(tile, stage).wait_send()
            send_left(tile, stage).wait_send()

    for made in sends:
        made.wait_send()


def shards(a_blocks, a_scale, a_rows, a_cols, b_blocks, b_scale, b_cols, c_rows, c_cols):
    edge = a_blocks.shape[1]
    half = edge // 2
    a_cap, c_cap = a_blocks.shape[0], c_rows.shape[0]
    per, kb = b_blocks.shape[0], b_blocks.shape[3]
    n_r, n_y, n_x = lax.axis_size("row"), lax.axis_size("col"), lax.axis_size("depth")
    dims = (n_x, n_y, n_r, a_cap, per, kb, c_cap)
    n_c = n_y * a_cap
    half_c = c_cap // 2

    width = -(-kb * n_c // LANES) * LANES

    dtype = a_blocks.dtype
    block, part = (edge, edge), (edge, half)
    dma = pltpu.SemaphoreType.DMA
    hops = n_r // 4
    n_meta = (n_y - 1) + (n_x - 1) + 1 + 4 * hops + 2
    n_units = 2 * kb + per
    n_ring = 2 * hops * n_units
    rows = (half, edge)
    tile = (half, half)
    any_space = pl.BlockSpec(memory_space=pl.ANY)
    vmem = pl.BlockSpec(memory_space=pltpu.VMEM)
    return pl.pallas_call(
        functools.partial(kernel, dims),
        out_shape=jax.ShapeDtypeStruct((c_cap,) + block, dtype),
        in_specs=[any_space, any_space] + [vmem] * 7,
        out_specs=any_space,
        scratch_shapes=[pltpu.VMEM((n_c,) + rows, dtype)] * 4
        + [
            pltpu.VMEM((n_r * kb,) + part, dtype),
            pltpu.VMEM((n_r * kb,) + part, dtype),
            pltpu.VMEM((n_r * per * kb,) + part, dtype),
            pltpu.VMEM((per, kb) + block, dtype),
            pltpu.VMEM((per, kb) + part, dtype),
            pltpu.VMEM((8, LANES), F32),
            pltpu.VMEM((n_x, 8, LANES), F32),
            pltpu.VMEM((2, n_y, 8, LANES), F32),
            pltpu.VMEM((2, n_r, 8, LANES), F32),
        ]
        + [
            space((8, width), kind)
            for _ in range(2)
            for space in (pltpu.VMEM, pltpu.SMEM)
            for kind in (jnp.int32, F32)
        ]
        + [pltpu.VMEM(tile, F32)]
        + [pltpu.VMEM((kb * n_c + 1,) + tile, dtype)] * 8
        + [pltpu.VMEM((12 * (half_c // 2),) + tile, dtype)] * 4
        + [pltpu.VMEM((4 * half_c,) + tile, dtype)] * 2
        + [pltpu.VMEM((2 * half_c,) + tile, dtype)] * 2
        + [
            pltpu.VMEM((c_cap,) + block, dtype),
            dma((7,)),
            dma((n_meta,)),
            dma((n_meta,)),
            dma((n_ring,)),
            dma((n_ring,)),
            dma((n_units + n_ring,)),
            dma((n_units + n_ring,)),
            dma((per,)),
            dma((per,)),
            dma((28,)),
            dma((28,)),
        ]
        + [dma((12,))] * 4
        + [dma((8,))] * 2
        + [dma((4,))] * 2
        + [dma((8,))],
        compiler_params=pltpu.CompilerParams(
            collective_id=0, has_side_effects=True, vmem_limit_bytes=62 * 1024 * 1024
        ),
    )(
        a_blocks,
        b_blocks.reshape(per, kb, edge, edge),
        a_scale.reshape(1, a_cap),
        a_rows.reshape(1, a_cap),
        a_cols.reshape(1, a_cap),
        b_scale.reshape(per, kb),
        b_cols.reshape(per, kb),
        c_rows.reshape(1, c_cap),
        c_cols.reshape(1, c_cap),
    )


def solution(mesh):
    return jax.shard_map(
        shards,
        mesh=mesh,
        in_specs=(
            P(("row", "col", "depth"), None, None),
            P(("row", "col", "depth")),
            P(("row", "col", "depth")),
            P(("row", "col", "depth")),
            P("row", "col", "depth", None, None, None),
            P("row", "col", "depth", None),
            P("row", "col", "depth", None),
            P(("row", "col", "depth")),
            P(("row", "col", "depth")),
        ),
        out_specs=P(("row", "col", "depth"), None, None),
        check_vma=False,
    )
```

time: 130 us -> 126 us (0.969)
  Pallas kernels: 125 us -> 122 us
    pallas_call x1, Pallas kernels: 125 us -> 122 us  [shards(): pl.pallas_call(functools.partial(kernel, dims), out_shape=jax.ShapeDtypeS...]
where the time goes in v4:
time: 126 us
  Pallas kernels  122 us (97%)
  local copies, waits for them, and re-layouts  3.47 us (3%)
    pallas_call x1, Pallas kernels, shards(): pl.pallas_call(functools.partial(kernel, dims), out_shape=jax.ShapeDtypeS...  122 us
    unnamed x1, local copies, waits for them, and re-layouts  3.47 us

profile of v4, /device:TPU:1, one launch (start us, length us, event | category | flops | bytes accessed | tf_op | source)
XLA Modules:
  0.0 125.6 jit_solution(16761930376489962715)
XLA Ops:
  0.0 122.2 %shard_map.91 = bf16[20,256,256]{2,1,0:T(8,128)(2,1)} custom-call(bf16[8,256,256]{2,1,0:T(8,128)(2,1)} %a_hbm.1, bf16[2,3,256,256]{3,2,1,0:T(8,128)(2,1)} %bitcast.8, f32[1,8]{1,0:T(1,128)} %bitcast.11, s32[1,8]{1,0:T(1,128)} %bitcast.12, s32[1,8]{1,0:T(1,128)} %bitcast.13, f32[2,3]{1,0:T(2,128)} %bitcast.9, s32[2,3]{1,0:T(2,128)} %bitcast.10, ...), custom_call_target="tpu_custom_call" | custom-call | tf_op jit(solution)/shard_map/pallas_call | solution.py:675
  122.2 3.5 %copy.11 = bf16[20,256,256]{2,1,0:T(8,128)(2,1)} copy(bf16[20,256,256]{2,1,0:T(8,128)(2,1)} %shard_map.91) | data formatting | bytes 5242880

commit v5 on v4

--- a/solution.py
+++ b/solution.py
@@ -92,13 +92,19 @@
 
 
 def kernel(
-    dims, a_hbm, b_hbm, a_scale, a_rows, a_cols, b_scale, b_cols, c_rows, c_cols, out_hbm,
+    dims, a_hbm, b_hbm, *rest):
+    small, (out_hbm,), scratch = rest[:7], rest[7:8], rest[8:]
+    body(dims, a_hbm, b_hbm, small, out_hbm, scratch[:7], *scratch[7:])
+
+
+def body(
+    dims, a_hbm, b_hbm, small, out_hbm, tables,
     a_own0, a_own1, a_pair0, a_pair1, b_one, b_two, b_second, raw_own, raw_pair, meta, meta_x, meta_y, meta_z,
     tab_int1, tab_scale1, ids1, scales1, tab_int2, tab_scale2, ids2, scales2,
-    acc, prod0, prod1, prod2, prod3, prod4, prod5, prod6, prod7,
+    acc, prod0, prod1, prod2, prod3, own_first,
     to_right, to_left, from_left, from_right, to_mirror, from_mirror, to_pair, from_pair, result,
     local_sem, meta_send, meta_recv, ring_send, ring_recv, core_send, core_recv, raw_send, raw_recv, a_send, a_recv,
-    r_send, r_recv, l_send, l_recv, m_send, m_recv, p_send, p_recv, out_sem,
+    r_send, r_recv, l_send, l_recv, m_send, m_recv, p_send, p_recv, out_sem, small_sem,
 ):
     n_x, n_y, n_r, a_cap, per, kb, c_cap = dims
     n_z = n_r // 2
@@ -108,7 +114,7 @@
     quarter = half // 2
     a_own, a_pair = (a_own0, a_own1), (a_pair0, a_pair1)
     first_prod = ((prod0, prod1), (prod2, prod3))
-    own_prod, pair_prod = (prod4, prod5), (prod6, prod7)
+    own_prod, pair_prod = (prod0, prod1), (prod2, prod3)
     row, col, dep = lax.axis_index("row"), lax.axis_index("col"), lax.axis_index("depth")
     z, core = row // 2, row % 2
 
@@ -128,7 +134,16 @@
     second_cols = pl.ds(half, half)
     low_lanes = iota((1, half), 1) < quarter
 
+    local_raw = pltpu.make_async_copy(b_hbm, raw_own, local_sem.at[0])
+    local_raw.start()
+    loads = [pltpu.make_async_copy(src, dst, small_sem.at[i]) for i, (src, dst) in enumerate(zip(small, tables))]
+    for made in loads:
+        made.start()
+    a_scale, a_rows, a_cols, b_scale, b_cols, c_rows, c_cols = tables
+
     meta[...] = jnp.zeros_like(meta)
+    for made in loads:
+        made.wait()
     meta[0:1, 0:a_cap] = a_scale[...]
     meta[1:2, 0:a_cap] = a_rows[...].astype(F32)
     meta[2:3, 0:a_cap] = a_cols[...].astype(F32)
@@ -140,13 +155,16 @@
     partners = [sibling, at_z(1), at_z(-1)] + [at_y(j) for j in range(1, n_y)] + [at_x(j) for j in range(1, n_x)]
     for partner in partners:
         pl.semaphore_signal(barrier, inc=1, device_id=partner, device_id_type=MESH)
-    local_raw = pltpu.make_async_copy(b_hbm, raw_own, local_sem.at[0])
-    local_raw.start()
     local_raw.wait()
-    for t in range(kb):
-        one, two = raw_own[0, t, :, 0:half].astype(F32), raw_own[1, t, :, 0:half].astype(F32)
-        b_one[row * kb + t] = jnp.where(low_lanes, one, pltpu.roll(two, quarter, 1)).astype(b_one.dtype)
-        b_two[row * kb + t] = jnp.where(low_lanes, pltpu.roll(one, quarter, 1), two).astype(b_two.dtype)
+
+    def pack_first(refs, number):
+        for t in range(kb):
+            one, two = raw_own[0, t, :, 0:half].astype(F32), raw_own[1, t, :, 0:half].astype(F32)
+            one = pltpu.roll(one, quarter, 1) if number else one
+            two = two if number else pltpu.roll(two, quarter, 1)
+            refs[row * kb + t] = jnp.where(low_lanes, one, two).astype(refs.dtype)
+
+    pack_first(b_one, 0)
     pl.semaphore_wait(barrier, len(partners))
 
     sends = []
@@ -216,7 +234,7 @@
     for unit in unit_one:
         send_first(b_unit(z, core, unit), unit)
     for inner in range(per):
-        push(raw_own.at[inner, :, :, second_cols], raw_pair.at[inner], raw_send.at[inner], raw_recv.at[inner], pair)
+        push(b_hbm.at[inner, :, :, second_cols], raw_pair.at[inner], raw_send.at[inner], raw_recv.at[inner], pair)
 
     mid = a_cap // 2
     y_up, y_down = at_y(1), at_y(-1)
@@ -438,6 +456,12 @@
 
         send_left(tile, 2).start()
 
+    def keep_own(tile):
+        @pl.loop(0, pairs)
+        def _(i):
+            own_first[tile * half_c + i] = first_block(tile, dep, 0, i)
+            own_first[tile * half_c + pairs + i] = first_block(tile, dep, half_c, i)
+
     def first_results(rr):
         tiles = (rr, 2 + rr)
         rows = slice(rr * half, (rr + 1) * half)
@@ -445,12 +469,12 @@
             for stage in (1, 2):
                 wait_right(tile, stage)
                 wait_left(tile, stage)
-        for base, left_stage, right_stage in ((0, 2, 1), (half_c, 1, 2)):
+        for base, kept, left_stage, right_stage in ((0, 0, 2, 1), (half_c, pairs, 1, 2)):
 
             @pl.loop(0, pairs)
             def _(i):
                 one, two = [
-                    first_block(tile, dep, base, i)
+                    own_first[tile * half_c + kept + i]
                     + from_left[(tile * 3 + left_stage) * pairs + i].astype(F32)
                     + from_right[(tile * 3 + right_stage) * pairs + i].astype(F32)
                     for tile in tiles
@@ -534,104 +558,109 @@
             for made in write(rr, k):
                 made.start()
 
+    forward_meta(0)
+    pack_first(b_two, 1)
+    send_first(b_unit(z, core, unit_two[1]), unit_two[1])
     forward_b(0, unit_one[0])
+    forward_b(0, unit_one[2])
     forward_b(0, unit_one[1])
-    forward_b(0, unit_one[2])
-    forward_meta(0)
-    pack(0)
+    forward_b(1, unit_one[0])
+    forward_b(1, unit_one[2])
     across_a(a_own, 0, 0)
     send_first(b_unit(z, core, unit_two[0]), unit_two[0])
+    forward_meta(1)
     send_first(b_unit(z, core, unit_two[2]), unit_two[2])
-    forward_meta(1)
-    send_first(b_unit(z, core, unit_two[1]), unit_two[1])
+    send_own_a(1)
+    pack(1)
+    send_raw_a(1)
+    forward_b(1, unit_one[1])
+    forward_b(2, unit_one[2])
     forward_b(0, unit_two[0])
     forward_meta(2)
-    forward_b(1, unit_one[1])
-    forward_b(1, unit_one[2])
-    pack(1)
-    send_own_a(1)
+    forward_b(2, unit_one[0])
+    forward_b(2, unit_one[1])
+    forward_b(0, unit_two[1])
     forward_b(0, unit_two[2])
+    forward_b(3, unit_one[0])
     forward_meta(3)
-    forward_b(1, unit_one[0])
-    forward_b(0, unit_two[1])
-    forward_b(2, unit_one[1])
+    pair_tables()
+    forward_b(1, unit_two[0])
+    forward_b(3, unit_one[1])
+    pack(0)
+    table1 = plan(0, tab_int1, tab_scale1, ids1, scales1, 3)
+    send_first(b_unit(z, core, unit_second[0]), unit_second[0])
     rest_a(a_own, 0, 0)
-    send_raw_a(1)
-    forward_b(1, unit_two[0])
-    forward_b(2, unit_one[2])
-    forward_b(2, unit_one[0])
-    pair_tables()
-    table1 = plan(0, tab_int1, tab_scale1, ids1, scales1, 3)
-    forward_b(3, unit_one[1])
-    send_first(b_unit(z, core, unit_second[0]), unit_second[0])
     forward_b(1, unit_two[2])
     forward_b(3, unit_one[2])
+    finish(unit_one[1])
     forward_b(1, unit_two[1])
+    forward_b(2, unit_two[0])
     across_a(a_own, 1, 0)
-    finish(unit_one[1])
-    forward_b(2, unit_two[0])
-    forward_b(3, unit_one[0])
+    finish(unit_one[0])
+    finish(unit_one[2])
     for made in table1 + local:
         made.wait()
-    finish(unit_one[2])
     send_first(b_unit(z, core, unit_second[1]), unit_second[1])
-    spread_pair_a(0)
-    finish(unit_one[0])
     multiply(a_own[0], b_one, ids1, scales1, prod0, True)
     first_sends(0)
+    spread_pair_a(1)
+    spread_pair_a(0)
+    forward_b(2, unit_two[2])
     forward_b(2, unit_two[1])
-    forward_b(2, unit_two[2])
-    spread_pair_a(1)
     forward_b(0, unit_second[0])
     rest_a(a_own, 1, 0)
     multiply(a_own[1], b_one, ids1, scales1, prod1, True)
     first_sends(1)
+    forward_b(0, unit_second[1])
     forward_b(3, unit_two[2])
-    finish(unit_two[2])
     pass_sums(0)
     forward_b(3, unit_two[0])
-    forward_b(0, unit_second[1])
+    finish(unit_two[0])
     forward_b(3, unit_two[1])
-    finish(unit_two[0])
-    forward_b(1, unit_second[0])
-    finish(unit_two[1])
-    multiply(a_own[1], b_two, ids1, scales1, prod3, True)
-    first_sends(3)
-    across_a(a_pair, 0, 6)
-    forward_b(1, unit_second[1])
-    multiply(a_own[0], b_two, ids1, scales1, prod2, True)
-    forward_b(2, unit_second[0])
-    first_sends(2)
-    pass_sums(1)
-    forward_b(2, unit_second[1])
+    across_a(a_pair, 1, 6)
+    keep_own(1)
     pulled(meta_y.at[1], meta_send.at[pair_meta], meta_recv.at[pair_meta])
     pulled(meta_z.at[1], meta_send.at[pair_meta + 1], meta_recv.at[pair_meta + 1])
     table2 = plan(1, tab_int2, tab_scale2, ids2, scales2, 5)
+    forward_b(1, unit_second[0])
+    pass_sums(1)
+    finish(unit_two[2])
+    finish(unit_two[1])
+    forward_b(1, unit_second[1])
+    multiply(a_own[0], b_two, ids1, scales1, prod2, True)
+    first_sends(2)
+    across_a(a_pair, 0, 6)
+    multiply(a_own[1], b_two, ids1, scales1, prod3, True)
+    forward_b(2, unit_second[1])
+    keep_own(0)
+    forward_b(2, unit_second[0])
+    first_sends(3)
+    keep_own(3)
+    forward_b(3, unit_second[1])
+    rest_a(a_pair, 1, 6)
+    pass_sums(2)
+    finish(unit_second[1])
+    forward_b(3, unit_second[0])
     pass_sums(3)
-    across_a(a_pair, 1, 6)
-    forward_b(3, unit_second[0])
-    forward_b(3, unit_second[1])
-    finish(unit_second[0])
     for made in table2:
         made.wait()
-    finish(unit_second[1])
-    multiply(a_own[0], b_second, ids1, scales1, prod4, False)
-    rest_a(a_pair, 0, 6)
-    pass_sums(2)
-    multiply(a_pair[0], b_second, ids2, scales2, prod6, False)
-    rest_a(a_pair, 1, 6)
-    second_sends(0, 0)
-    first_results(1)
-    second_sends(0, 1)
-    multiply(a_pair[1], b_second, ids2, scales2, prod7, False)
-    multiply(a_own[1], b_second, ids1, scales1, prod5, False)
-    second_sums(0)
+    finish(unit_second[0])
+    multiply(a_own[1], b_second, ids1, scales1, prod1, False)
+    multiply(a_pair[1], b_second, ids2, scales2, prod3, False)
     second_sends(1, 0)
     second_sends(1, 1)
+    keep_own(2)
+    rest_a(a_pair, 0, 6)
+    multiply(a_pair[0], b_second, ids2, scales2, prod2, False)
+    multiply(a_own[0], b_second, ids1, scales1, prod0, False)
+    second_sends(0, 0)
+    second_sends(0, 1)
     first_results(0)
     second_sums(1)
+    second_sums(0)
+    first_results(1)
+    second_results(1)
     second_results(0)
-    second_results(1)
 
     for rr in range(2):
         for k in range(2):
@@ -671,13 +700,16 @@
     rows = (half, edge)
     tile = (half, half)
     any_space = pl.BlockSpec(memory_space=pl.ANY)
-    vmem = pl.BlockSpec(memory_space=pltpu.VMEM)
-    return pl.pallas_call(
+    small = [v.reshape(1, a_cap) for v in (a_scale, a_rows, a_cols)]
+    small += [v.reshape(per, kb) for v in (b_scale, b_cols)]
+    small += [v.reshape(1, c_cap) for v in (c_rows, c_cols)]
+    gathered = pl.pallas_call(
         functools.partial(kernel, dims),
         out_shape=jax.ShapeDtypeStruct((c_cap,) + block, dtype),
-        in_specs=[any_space, any_space] + [vmem] * 7,
+        in_specs=[any_space] * 9,
         out_specs=any_space,
-        scratch_shapes=[pltpu.VMEM((n_c,) + rows, dtype)] * 4
+        scratch_shapes=[pltpu.VMEM(v.shape, v.dtype) for v in small]
+        + [pltpu.VMEM((n_c,) + rows, dtype)] * 4
         + [
             pltpu.VMEM((n_r * kb,) + part, dtype),
             pltpu.VMEM((n_r * kb,) + part, dtype),
@@ -696,7 +728,8 @@
             for kind in (jnp.int32, F32)
         ]
         + [pltpu.VMEM(tile, F32)]
-        + [pltpu.VMEM((kb * n_c + 1,) + tile, dtype)] * 8
+        + [pltpu.VMEM((kb * n_c + 1,) + tile, dtype)] * 4
+        + [pltpu.VMEM((4 * half_c,) + tile, F32)]
         + [pltpu.VMEM((12 * (half_c // 2),) + tile, dtype)] * 4
         + [pltpu.VMEM((4 * half_c,) + tile, dtype)] * 2
         + [pltpu.VMEM((2 * half_c,) + tile, dtype)] * 2
@@ -717,21 +750,40 @@
         + [dma((12,))] * 4
         + [dma((8,))] * 2
         + [dma((4,))] * 2
-        + [dma((8,))],
+        + [dma((8,))]
+        + [dma((7,))],
         compiler_params=pltpu.CompilerParams(
             collective_id=0, has_side_effects=True, vmem_limit_bytes=62 * 1024 * 1024
         ),
     )(
         a_blocks,
         b_blocks.reshape(per, kb, edge, edge),
-        a_scale.reshape(1, a_cap),
-        a_rows.reshape(1, a_cap),
-        a_cols.reshape(1, a_cap),
-        b_scale.reshape(per, kb),
-        b_cols.reshape(per, kb),
-        c_rows.reshape(1, c_cap),
-        c_cols.reshape(1, c_cap),
+        *small,
     )
+    copies = 10
+    return pl.pallas_call(
+        hand_over,
+        out_shape=jax.ShapeDtypeStruct(gathered.shape, dtype),
+        in_specs=[any_space],
+        out_specs=any_space,
+        scratch_shapes=[pltpu.VMEM(gathered.shape, dtype), dma((copies,)), dma((copies,))],
+        compiler_params=pltpu.CompilerParams(vmem_limit_bytes=62 * 1024 * 1024),
+    )(gathered)
+
+
+def hand_over(src, dst, held, in_sems, out_sems):
+    copies = in_sems.shape[0]
+    size = src.shape[0] // copies
+    parts = [pl.ds(i * size, size) for i in range(copies)]
+    reads = [pltpu.make_async_copy(src.at[p], held.at[p], in_sems.at[i]) for i, p in enumerate(parts)]
+    writes = [pltpu.make_async_copy(held.at[p], dst.at[p], out_sems.at[i]) for i, p in enumerate(parts)]
+    for one in reads:
+        one.start()
+    for read, write in zip(reads, writes):
+        read.wait()
+        write.start()
+    for one in writes:
+        one.wait()
 
 
 def solution(mesh):

time: 126 us -> 123 us (0.976)
  local copies, waits for them, and re-layouts: 3.47 us -> 0 us
    unnamed x1 -> x0, local copies, waits for them, and re-layouts: 3.47 us -> none
    pallas_call x0 -> x1, Pallas kernels: none -> 2.6 us  [shards(): pl.pallas_call(hand_over, out_shape=jax.ShapeDtypeStruct(gathered.shape,...]
    pallas_call x1, Pallas kernels: 122 us -> 120 us  [shards(): pl.pallas_call(functools.partial(kernel, dims), out_shape=jax.ShapeDtypeS...]
where the time goes in v5:
time: 123 us
  Pallas kernels  123 us (100%)
    pallas_call x1, Pallas kernels, shards(): pl.pallas_call(functools.partial(kernel, dims), out_shape=jax.ShapeDtypeS...  120 us
    pallas_call x1, Pallas kernels, shards(): pl.pallas_call(hand_over, out_shape=jax.ShapeDtypeStruct(gathered.shape,...  2.6 us

profile of v5, /device:TPU:1, one launch (start us, length us, event | category | flops | bytes accessed | tf_op | source)
XLA Modules:
  0.0 122.9 jit_solution(15293454627638988942)
XLA Ops:
  0.0 120.2 %shard_map.91.src = bf16[20,256,256]{2,1,0:T(8,128)(2,1)} custom-call(bf16[8,256,256]{2,1,0:T(8,128)(2,1)} %a_hbm.1, bf16[2,3,256,256]{3,2,1,0:T(8,128)(2,1)} %bitcast.8, f32[1,8]{1,0:T(1,128)} %bitcast.11, s32[1,8]{1,0:T(1,128)} %bitcast.12, s32[1,8]{1,0:T(1,128)} %bitcast.13, f32[2,3]{1,0:T(2,128)} %bitcast.9, s32[2,3]{1,0:T(2,128)} %bitcast.10, ...), custom_call_target="tpu_custom_call" | custom-call | tf_op jit(solution)/shard_map/pallas_call | solution.py:706
  120.3 2.6 %shard_map.92 = bf16[20,256,256]{2,1,0:T(8,128)(2,1)} custom-call(bf16[20,256,256]{2,1,0:T(8,128)(2,1)} %shard_map.91.src), custom_call_target="tpu_custom_call" | custom-call | tf_op jit(solution)/shard_map/pallas_call | solution.py:764

commit v6 on v5

--- a/solution.py
+++ b/solution.py
@@ -362,7 +362,7 @@
         acc[...] = jnp.zeros_like(acc)
         prod[n_p] = jnp.zeros(prod.shape[1:], prod.dtype)
 
-        @pl.loop(0, n_p, unroll=16)
+        @pl.loop(0, n_p, unroll=32)
         def _(j):
             left_block = a_refs[bounded(ids[0, j], n_c)]
             right_block = b_refs[bounded(ids[3 if split else 1, j], b_refs.shape[0])]
@@ -413,25 +413,25 @@
     def first_sends(tile):
         at = tile * 3 * pairs
 
-        @pl.loop(0, pairs)
+        @pl.loop(0, pairs, unroll=pairs)
         def _(i):
             to_right[at + i] = first_block(tile, d_far, 0, i).astype(dtype)
 
         send_right(tile, 0).start()
 
-        @pl.loop(0, pairs)
+        @pl.loop(0, pairs, unroll=pairs)
         def _(i):
             to_left[at + i] = first_block(tile, d_far, half_c, i).astype(dtype)
 
         send_left(tile, 0).start()
 
-        @pl.loop(0, pairs)
+        @pl.loop(0, pairs, unroll=pairs)
         def _(i):
             to_right[at + pairs + i] = first_block(tile, d_right, half_c, i).astype(dtype)
 
         send_right(tile, 1).start()
 
-        @pl.loop(0, pairs)
+        @pl.loop(0, pairs, unroll=pairs)
         def _(i):
             to_left[at + pairs + i] = first_block(tile, d_left, 0, i).astype(dtype)
 
@@ -441,7 +441,7 @@
         at = tile * 3 * pairs
         wait_left(tile, 0)
 
-        @pl.loop(0, pairs)
+        @pl.loop(0, pairs, unroll=pairs)
         def _(i):
             total = first_block(tile, d_right, 0, i) + from_left[at + i].astype(F32)
             to_right[at + 2 * pairs + i] = total.astype(dtype)
@@ -449,7 +449,7 @@
         send_right(tile, 2).start()
         wait_right(tile, 0)
 
-        @pl.loop(0, pairs)
+        @pl.loop(0, pairs, unroll=pairs)
         def _(i):
             total = first_block(tile, d_left, half_c, i) + from_right[at + i].astype(F32)
             to_left[at + 2 * pairs + i] = total.astype(dtype)
@@ -457,7 +457,7 @@
         send_left(tile, 2).start()
 
     def keep_own(tile):
-        @pl.loop(0, pairs)
+        @pl.loop(0, pairs, unroll=pairs)
         def _(i):
             own_first[tile * half_c + i] = first_block(tile, dep, 0, i)
             own_first[tile * half_c + pairs + i] = first_block(tile, dep, half_c, i)
@@ -471,7 +471,7 @@
                 wait_left(tile, stage)
         for base, kept, left_stage, right_stage in ((0, 0, 2, 1), (half_c, pairs, 1, 2)):
 
-            @pl.loop(0, pairs)
+            @pl.loop(0, pairs, unroll=pairs)
             def _(i):
                 one, two = [
                     own_first[tile * half_c + kept + i]
@@ -508,7 +508,7 @@
         dest = (d_far, d_mirror)[stage]
         for k in range(2):
 
-            @pl.loop(0, pairs)
+            @pl.loop(0, pairs, unroll=pairs)
             def _(i):
                 u = k * pairs + i
                 to_mirror[(rr * 2 + stage) * half_c + u] = packed(rr, dest, u).astype(dtype)
@@ -519,7 +519,7 @@
         for k in range(2):
             send_mirror(rr, 0, k).wait_recv()
 
-            @pl.loop(0, pairs)
+            @pl.loop(0, pairs, unroll=pairs)
             def _(i):
                 u = k * pairs + i
                 total = packed(rr, d_pair, u) + from_mirror[rr * 2 * half_c + u].astype(F32)
@@ -543,7 +543,7 @@
             send_pair(rr, k).wait_recv()
             send_mirror(rr, 1, k).wait_recv()
 
-            @pl.loop(0, pairs)
+            @pl.loop(0, pairs, unroll=pairs)
             def _(i):
                 u = k * pairs + i
                 mine = packed(rr, dep, u) + from_mirror[(rr * 2 + 1) * half_c + u].astype(F32)
@@ -560,106 +560,106 @@
 
     forward_meta(0)
     pack_first(b_two, 1)
+    forward_b(0, unit_one[0])
+    forward_b(0, unit_one[1])
+    forward_b(0, unit_one[2])
+    send_first(b_unit(z, core, unit_two[0]), unit_two[0])
     send_first(b_unit(z, core, unit_two[1]), unit_two[1])
-    forward_b(0, unit_one[0])
-    forward_b(0, unit_one[2])
-    forward_b(0, unit_one[1])
-    forward_b(1, unit_one[0])
+    forward_b(1, unit_one[1])
+    forward_meta(1)
+    pack(0)
     forward_b(1, unit_one[2])
     across_a(a_own, 0, 0)
-    send_first(b_unit(z, core, unit_two[0]), unit_two[0])
-    forward_meta(1)
-    send_first(b_unit(z, core, unit_two[2]), unit_two[2])
-    send_own_a(1)
-    pack(1)
-    send_raw_a(1)
-    forward_b(1, unit_one[1])
-    forward_b(2, unit_one[2])
+    forward_b(1, unit_one[0])
     forward_b(0, unit_two[0])
     forward_meta(2)
+    send_first(b_unit(z, core, unit_two[2]), unit_two[2])
+    pack(1)
+    forward_b(2, unit_one[2])
+    forward_b(2, unit_one[1])
+    send_own_a(1)
+    forward_b(0, unit_two[1])
+    forward_b(1, unit_two[0])
     forward_b(2, unit_one[0])
-    forward_b(2, unit_one[1])
-    forward_b(0, unit_two[1])
+    forward_meta(3)
     forward_b(0, unit_two[2])
+    send_raw_a(1)
+    rest_a(a_own, 0, 0)
+    send_first(b_unit(z, core, unit_second[0]), unit_second[0])
+    pair_tables()
+    forward_b(3, unit_one[2])
+    forward_b(1, unit_two[1])
+    forward_b(3, unit_one[1])
+    finish(unit_one[2])
+    table1 = plan(0, tab_int1, tab_scale1, ids1, scales1, 3)
+    finish(unit_one[1])
+    across_a(a_own, 1, 0)
     forward_b(3, unit_one[0])
-    forward_meta(3)
-    pair_tables()
-    forward_b(1, unit_two[0])
-    forward_b(3, unit_one[1])
-    pack(0)
-    table1 = plan(0, tab_int1, tab_scale1, ids1, scales1, 3)
-    send_first(b_unit(z, core, unit_second[0]), unit_second[0])
-    rest_a(a_own, 0, 0)
     forward_b(1, unit_two[2])
-    forward_b(3, unit_one[2])
-    finish(unit_one[1])
-    forward_b(1, unit_two[1])
-    forward_b(2, unit_two[0])
-    across_a(a_own, 1, 0)
-    finish(unit_one[0])
-    finish(unit_one[2])
     for made in table1 + local:
         made.wait()
+    spread_pair_a(0)
+    finish(unit_one[0])
+    forward_b(2, unit_two[0])
     send_first(b_unit(z, core, unit_second[1]), unit_second[1])
     multiply(a_own[0], b_one, ids1, scales1, prod0, True)
     first_sends(0)
-    spread_pair_a(1)
-    spread_pair_a(0)
+    forward_b(2, unit_two[1])
     forward_b(2, unit_two[2])
-    forward_b(2, unit_two[1])
     forward_b(0, unit_second[0])
     rest_a(a_own, 1, 0)
     multiply(a_own[1], b_one, ids1, scales1, prod1, True)
     first_sends(1)
     forward_b(0, unit_second[1])
-    forward_b(3, unit_two[2])
+    spread_pair_a(1)
+    forward_b(3, unit_two[1])
     pass_sums(0)
-    forward_b(3, unit_two[0])
-    finish(unit_two[0])
-    forward_b(3, unit_two[1])
-    across_a(a_pair, 1, 6)
-    keep_own(1)
     pulled(meta_y.at[1], meta_send.at[pair_meta], meta_recv.at[pair_meta])
     pulled(meta_z.at[1], meta_send.at[pair_meta + 1], meta_recv.at[pair_meta + 1])
     table2 = plan(1, tab_int2, tab_scale2, ids2, scales2, 5)
+    forward_b(3, unit_two[0])
     forward_b(1, unit_second[0])
+    forward_b(3, unit_two[2])
+    finish(unit_two[0])
     pass_sums(1)
     finish(unit_two[2])
     finish(unit_two[1])
     forward_b(1, unit_second[1])
     multiply(a_own[0], b_two, ids1, scales1, prod2, True)
     first_sends(2)
-    across_a(a_pair, 0, 6)
+    forward_b(2, unit_second[0])
+    across_a(a_pair, 1, 6)
     multiply(a_own[1], b_two, ids1, scales1, prod3, True)
     forward_b(2, unit_second[1])
-    keep_own(0)
-    forward_b(2, unit_second[0])
-    first_sends(3)
-    keep_own(3)
-    forward_b(3, unit_second[1])
-    rest_a(a_pair, 1, 6)
-    pass_sums(2)
-    finish(unit_second[1])
-    forward_b(3, unit_second[0])
-    pass_sums(3)
     for made in table2:
         made.wait()
+    keep_own(0)
+    first_sends(3)
+    pass_sums(2)
+    forward_b(3, unit_second[0])
+    keep_own(2)
+    keep_own(1)
+    rest_a(a_pair, 1, 6)
     finish(unit_second[0])
+    across_a(a_pair, 0, 6)
+    forward_b(3, unit_second[1])
+    pass_sums(3)
+    finish(unit_second[1])
     multiply(a_own[1], b_second, ids1, scales1, prod1, False)
+    keep_own(3)
     multiply(a_pair[1], b_second, ids2, scales2, prod3, False)
     second_sends(1, 0)
+    multiply(a_own[0], b_second, ids1, scales1, prod0, False)
     second_sends(1, 1)
-    keep_own(2)
+    first_results(0)
+    second_sums(1)
     rest_a(a_pair, 0, 6)
     multiply(a_pair[0], b_second, ids2, scales2, prod2, False)
-    multiply(a_own[0], b_second, ids1, scales1, prod0, False)
     second_sends(0, 0)
     second_sends(0, 1)
-    first_results(0)
-    second_sums(1)
-    second_sums(0)
     first_results(1)
     second_results(1)
+    second_sums(0)
     second_results(0)
 
     for rr in range(2):

time: 123 us -> 121 us (0.984)
  Pallas kernels: 123 us -> 121 us
    pallas_call x1, Pallas kernels: 120 us -> 118 us  [shards(): pl.pallas_call(functools.partial(kernel, dims), out_shape=jax.ShapeDtypeS...]
where the time goes in v6:
time: 121 us
  Pallas kernels  121 us (100%)
    pallas_call x1, Pallas kernels, shards(): pl.pallas_call(functools.partial(kernel, dims), out_shape=jax.ShapeDtypeS...  118 us
    pallas_call x1, Pallas kernels, shards(): pl.pallas_call(hand_over, out_shape=jax.ShapeDtypeStruct(gathered.shape,...  2.6 us

profile of v6, /device:TPU:1, one launch (start us, length us, event | category | flops | bytes accessed | tf_op | source)
XLA Modules:
  0.0 120.8 jit_solution(10214775894388749388)
XLA Ops:
  0.0 118.1 %shard_map.91.src = bf16[20,256,256]{2,1,0:T(8,128)(2,1)} custom-call(bf16[8,256,256]{2,1,0:T(8,128)(2,1)} %a_hbm.1, bf16[2,3,256,256]{3,2,1,0:T(8,128)(2,1)} %bitcast.8, f32[1,8]{1,0:T(1,128)} %bitcast.11, s32[1,8]{1,0:T(1,128)} %bitcast.12, s32[1,8]{1,0:T(1,128)} %bitcast.13, f32[2,3]{1,0:T(2,128)} %bitcast.9, s32[2,3]{1,0:T(2,128)} %bitcast.10, ...), custom_call_target="tpu_custom_call" | custom-call | tf_op jit(solution)/shard_map/pallas_call | solution.py:706
  118.1 2.6 %shard_map.92 = bf16[20,256,256]{2,1,0:T(8,128)(2,1)} custom-call(bf16[20,256,256]{2,1,0:T(8,128)(2,1)} %shard_map.91.src), custom_call_target="tpu_custom_call" | custom-call | tf_op jit(solution)/shard_map/pallas_call | solution.py:764
